TPU v7x, 32 devices: a whole 2x2x4 slice. The times are simulated.
32 devices in a mesh: pipe: 4 (over x, core), expert: 8 (over z, y).
Axes of the slice: x: 2, y: 2, z: 4, core: 2. Of those that a mesh axis runs over, the one named last changes fastest.
Arguments:
- held: bfloat16 [4, 256, 2048], P('pipe', 'expert'), may hold values from -23 to 23
- fresh: bfloat16 [256, 2048], P('expert'), may hold values from -23 to 23
- routes: int32 [4, 256, 2], P('pipe', 'expert'), may hold values from 0 to 7, all different within a row; in each aligned block of 32 rows (0 to 31, 32 to 63, ..., all dimensions but the last counted through in order) at most 16 rows name the same one
- norm_gain: float32 [4, 2048], P('pipe'), may hold values from 0.25 to 1.75
- router: bfloat16 [4, 2048, 8], P('pipe'), may hold values from -0.125 to 0.125
- w_gate: bfloat16 [4, 8, 2048, 7168], P('pipe', 'expert'), may hold values from -0.125 to 0.125
- w_up: bfloat16 [4, 8, 2048, 7168], P('pipe', 'expert'), may hold values from -0.125 to 0.125
- w_down: bfloat16 [4, 8, 7168, 2048], P('pipe', 'expert'), may hold values from -0.0625 to 0.0625
Outputs:
- section_out: bfloat16 [4, 256, 2048], P('pipe', 'expert')
Inputs may be any that keep to these rules, and one draw needn't show every extreme that they name: `routes`: each token names two different experts; among the 32 tokens of one device at one section no expert is named more than 16 times, and in every draw some device's tokens name one expert exactly 16 times.
All inputs are finite; a program needn't handle non-finite values.
Results may differ from a plain program's by a relative error of at most 0.0045.
Values may be sent and summed in bfloat16 or wider, within the bound.
No kernel may reach another device: no remote copies, remote signals or barrier semaphores. Data moves between devices by JAX's collectives and lax.ppermute only.
A program may use at most 128 MiB of HBM per device.

v0:
```python
import jax
import jax.numpy as jnp
from jax import lax
from jax.sharding import PartitionSpec as P


def passed_along(x, axis, by):
    length = lax.axis_size(axis)
    pairs = [(i, i + by) for i in range(length) if 0 <= i + by < length]
    return lax.ppermute(x, axis, pairs)


def per_device(held, fresh, routes, norm_gain, router, w_gate, w_up, w_down):
    tok_rows = fresh.shape[0]
    model_width = fresh.shape[1]
    experts = router.shape[2]
    devices = lax.axis_size("expert")
    shard_count = devices // experts
    capacity = tok_rows // 2
    received = passed_along(held[0], "pipe", 1)
    section_index = lax.axis_index("pipe")
    inputs = jnp.where(section_index == 0, fresh, received)
    values = inputs.astype(jnp.float32)
    mean_square = jnp.mean(values * values, axis=-1, keepdims=True)
    normed = (values * lax.rsqrt(mean_square + 1e-05) * norm_gain[0]).astype(jnp.bfloat16)
    logits = jnp.dot(normed, router[0], preferred_element_type=jnp.float32)
    chosen = routes[0]
    expert_ids = jnp.arange(experts, dtype=jnp.int32)
    token_hits = (chosen[:, :, None] == expert_ids[None, None, :]).astype(jnp.float32)
    picked_logits = jnp.sum(token_hits * logits[:, None, :], axis=2)
    shares = jnp.stack(
        [
            jax.nn.sigmoid(picked_logits[:, 0] - picked_logits[:, 1]),
            jax.nn.sigmoid(picked_logits[:, 1] - picked_logits[:, 0]),
        ],
        axis=1,
    )
    flat_choice = chosen.reshape(-1)
    onehot = (flat_choice[:, None] == expert_ids[None, :]).astype(jnp.int32)
    rank_table = jnp.cumsum(onehot, axis=0) - 1
    slot_index = jnp.sum(onehot * rank_table, axis=1)
    target = flat_choice * capacity + slot_index
    slot_ids = jnp.arange(experts * capacity, dtype=jnp.int32)
    placing = (target[:, None] == slot_ids[None, :]).astype(jnp.bfloat16)
    placing_tok = jnp.sum(placing.reshape(tok_rows, 2, experts * capacity), axis=1)
    buffer = jnp.dot(placing_tok.T, normed, preferred_element_type=jnp.float32).astype(jnp.bfloat16)
    gate_matrix = w_gate[0, 0]
    up_matrix = w_up[0, 0]
    down_matrix = w_down[0, 0]
    outgoing = jnp.broadcast_to(
        buffer.reshape(experts, 1, capacity, model_width),
        (experts, shard_count, capacity, model_width),
    )
    outgoing = outgoing.reshape(devices, capacity, model_width)
    row_block = lax.all_to_all(outgoing, "expert", split_axis=0, concat_axis=0, tiled=True)
    flat_rows = row_block.reshape(-1, model_width)
    gate_proj = jnp.dot(flat_rows, gate_matrix, preferred_element_type=jnp.float32)
    up_proj = jnp.dot(flat_rows, up_matrix, preferred_element_type=jnp.float32)
    hidden = (jax.nn.silu(gate_proj) * up_proj).astype(jnp.bfloat16)
    partial_value = jnp.dot(hidden, down_matrix, preferred_element_type=jnp.float32).astype(
        jnp.bfloat16
    )
    came_back = lax.all_to_all(
        partial_value.reshape(row_block.shape), "expert", split_axis=0, concat_axis=0, tiled=True
    )
    expert_out = jnp.sum(
        came_back.reshape(experts, shard_count, capacity, model_width).astype(jnp.float32), axis=1
    ).astype(jnp.bfloat16)
    picked = jnp.dot(
        placing,
        expert_out.reshape(experts * capacity, model_width),
        preferred_element_type=jnp.float32,
    )
    picked = picked.reshape(tok_rows, 2, model_width)
    branch = shares[:, 0, None] * picked[:, 0] + shares[:, 1, None] * picked[:, 1]
    section_out = (values + branch).astype(jnp.bfloat16)
    return section_out[None]


def solution(mesh):
    in_specs = (
        P("pipe", "expert", None),
        P("expert", None),
        P("pipe", "expert", None),
        P("pipe", None),
        P("pipe", None, None),
        P("pipe", "expert", None, None),
        P("pipe", "expert", None, None),
        P("pipe", "expert", None, None),
    )
    out_specs = P("pipe", "expert", None)
    return jax.shard_map(
        per_device, mesh=mesh, in_specs=in_specs, out_specs=out_specs, check_vma=False
    )
```

profile of v0, /device:TPU:0, one launch (start us, length us, event | category | flops | bytes accessed | tf_op | source)
XLA Modules:
  0.0 86.4 jit_solution(7338840324082408850)
XLA Ops:
  0.0 0.0 copy-start
  0.0 2.5 %collective-permute-start = (bf16[32,2048]{1,0:T(8,128)(2,1)}, bf16[32,2048]{1,0:T(8,128)(2,1)S(1)}, u32[]{:S(2)}, u32[]{:S(2)}) collective-permute-start(bf16[32,2048]{1,0:T(8,128)(2,1)} %bitcast.70), channel_id=1, source_target_pairs={{0,8},{8,16},{16,24},{1,9},{9,17},{17,25},{2,10},{10,18},{18,26},{... | collective-permute-start | bytes 393224 | tf_op jit(solution)/shard_map/ppermute | solution.py:10
  2.5 0.8 copy.19
  3.3 0.1 eq.74
  3.4 0.1 fusion.32
  3.4 0.1 reduce_window_sum.11
  3.5 0.2 select_reduce_fusion
  3.7 0.1 reduce_sum.48
  3.8 0.1 copy.20
  3.9 0.7 multiply_add_fusion
  4.6 0.1 fusion.37
  4.7 0.0 collective-permute-done
  4.7 1.1 %fusion.20 = (f32[32]{0:T(128)S(1)}, bf16[32,2048]{1,0:T(8,128)(2,1)S(1)}) fusion(bf16[32,2048]{1,0:T(8,128)(2,1)} %param.9, bf16[32,2048]{1,0:T(8,128)(2,1)S(1)} %collective-permute-done, pred[]{:T(512)S(6)} %eq.69), kind=kLoop, calls=%fused_computation.14 | loop fusion | flops 262112 | bytes 393345 | tf_op jit(solution)/shard_map/reduce_sum | solution.py:24
  5.8 1.0 %convolution_convert_fusion = bf16[128,2048]{1,0:T(8,128)(2,1)S(1)} fusion(bf16[32,128]{1,0:T(8,128)(2,1)S(1)} %fusion.37, bf16[32,2048]{1,0:T(8,128)(2,1)S(1)} %get-tuple-element.6, f32[2048]{0:T(1024)} %bitcast.68, f32[32]{0:T(128)S(1)} %add_rsqrt_fusion), kind=kOutput, calls=%fused_computation.8 | convolution fusion | flops 17301504 | bytes 671872 | tf_op jit(solution)/shard_map/dot_general | solution.py:46
  6.8 22.0 %all_to_all.10 = bf16[8,16,2048]{2,1,0:T(8,128)(2,1)S(1)} all-to-all(bf16[8,16,2048]{2,1,0:T(8,128)(2,1)S(1)} %bitcast.66), channel_id=1, replica_groups=mesh['pipe'=4,'expert'=8] {'expert'}, dimensions={0} | all-to-all | bytes 1048576 | tf_op jit(solution)/shard_map/all_to_all | solution.py:55
  28.8 15.2 %fusion.4 = f32[128,7168]{1,0:T(8,128)} fusion(bf16[128,2048]{1,0:T(8,128)(2,1)S(1)} %bitcast.63, bf16[1,1,2048,7168]{3,2,1,0:T(8,128)(2,1)} %param.13), kind=kOutput, calls=%fused_computation.4 | convolution fusion | flops 3758096384 | bytes 33554432 | tf_op jit(solution)/shard_map/dot_general | solution.py:57
  44.0 0.0 copy-start.2
  44.0 0.0 copy-start.1
  44.0 23.0 %fusion.14 = bf16[128,2048]{1,0:T(8,128)(2,1)} fusion(bf16[1,1,7168,2048]{3,2,1,0:T(8,128)(2,1)} %param.15, bf16[128,2048]{1,0:T(8,128)(2,1)S(1)} %bitcast.64, bf16[1,1,2048,7168]{3,2,1,0:T(8,128)(2,1)} %param.14, f32[128,7168]{1,0:T(8,128)} %fusion.4), kind=kOutput, calls=%fused_computation.9 | convolution fusion | flops 7521959936 | bytes 63438848 | tf_op jit(solution)/shard_map/dot_general | solution.py:60
  67.0 3.6 %all-to-all-start.1 = ((bf16[8,16,2048]{2,1,0:T(8,128)(2,1)}), bf16[8,16,2048]{2,1,0:T(8,128)(2,1)S(1)}, u32[]{:S(2)}, u32[]{:S(2)}) async-start(bf16[8,16,2048]{2,1,0:T(8,128)(2,1)} %bitcast.11), calls=%async_computation.1 | async-start | bytes 1048576 | tf_op jit(solution)/shard_map/all_to_all | solution.py:63
  70.7 0.0 copy-done
  70.7 0.0 copy-done.2
  70.7 0.2 fusion.29
  70.9 0.0 copy-done.1
  70.9 14.5 %all-to-all-done.1 = bf16[8,16,2048]{2,1,0:T(8,128)(2,1)S(1)} async-done(((bf16[8,16,2048]{2,1,0:T(8,128)(2,1)}), bf16[8,16,2048]{2,1,0:T(8,128)(2,1)S(1)}, u32[]{:S(2)}, u32[]{:S(2)}) %all-to-all-start.1) | async-done | bytes 524320 | tf_op jit(solution)/shard_map/all_to_all | solution.py:63
  85.4 0.3 fusion.34
  85.7 0.8 fusion.27
  (3 shorter events, 0.0 us)
Async XLA Ops:
  0.0 70.7 %copy-start = (bf16[1,2048,8]{1,2,0:T(8,128)(2,1)S(1)}, bf16[1,2048,8]{1,2,0:T(8,128)(2,1)}, u32[]{:S(2)}) copy-start(bf16[1,2048,8]{1,2,0:T(8,128)(2,1)} %param.12) | copy-start | bytes 98308
  0.0 4.7 %collective-permute-start = (bf16[32,2048]{1,0:T(8,128)(2,1)}, bf16[32,2048]{1,0:T(8,128)(2,1)S(1)}, u32[]{:S(2)}, u32[]{:S(2)}) collective-permute-start(bf16[32,2048]{1,0:T(8,128)(2,1)} %bitcast.70), channel_id=1, source_target_pairs={{0,8},{8,16},{16,24},{1,9},{9,17},{17,25},{2,10},{10,18},{18,26},{... | collective-permute-start | bytes 393224 | tf_op jit(solution)/shard_map/ppermute | solution.py:10
  44.0 26.7 %copy-start.2 = (f32[1,2048]{1,0:T(1,128)S(1)}, f32[1,2048]{1,0:T(1,128)}, u32[]{:S(2)}) copy-start(f32[1,2048]{1,0:T(1,128)} %param.11) | copy-start | bytes 24580
  44.0 26.9 %copy-start.1 = (s32[1,32,2]{1,2,0:T(2,128)S(1)}, s32[1,32,2]{1,2,0:T(2,128)}, u32[]{:S(2)}) copy-start(s32[1,32,2]{1,2,0:T(2,128)} %param.10) | copy-start | bytes 772
  67.0 18.4 %all-to-all-start.1 = ((bf16[8,16,2048]{2,1,0:T(8,128)(2,1)}), bf16[8,16,2048]{2,1,0:T(8,128)(2,1)S(1)}, u32[]{:S(2)}, u32[]{:S(2)}) async-start(bf16[8,16,2048]{2,1,0:T(8,128)(2,1)} %bitcast.11), calls=%async_computation.1 | async-start | bytes 1048576 | tf_op jit(solution)/shard_map/all_to_all | solution.py:63
where the time goes:
time: 86.9 us; the launch traced here: 86.4 us
  matrix products  39.7 us (46%)
  blocking collectives  22 us (25%)
  waiting for transfers between devices  14.5 us (17%)
  starting transfers between devices  6.11 us (7%)
  other arithmetic  3.01 us (3%)
  local copies, waits for them, and re-layouts  1.06 us (1%)
    dot_general x1, matrix products, per_device(): jnp.dot(hidden, down_matrix, preferred_element_type=jnp.float32)  23 us
    all_to_all x1, blocking collectives, per_device(): lax.all_to_all(outgoing, 'expert', split_axis=0, concat_axis=0, tiled=True)  22 us
    dot_general x1, matrix products, per_device(): jnp.dot(flat_rows, gate_matrix, preferred_element_type=jnp.float32)  15.2 us
    all_to_all x1, waiting for transfers between devices, per_device(): lax.all_to_all(partial_value.reshape(row_block.shape), 'expert', split_ax...  14.5 us
    all_to_all x1, starting transfers between devices, per_device(): lax.all_to_all(partial_value.reshape(row_block.shape), 'expert', split_ax...  3.63 us
    ppermute x1, starting transfers between devices, passed_along(): return lax.ppermute(x, axis, pairs)  2.48 us
  transfers between devices with their start and end apart: 2, of which 1 were waited for; matrix products, arithmetic and copies ran while one was open for 3% of the time, Pallas kernels for 0%

commit v1 on v0

--- a/solution.py
+++ b/solution.py
@@ -1,7 +1,15 @@
+import functools
+
 import jax
 import jax.numpy as jnp
 from jax import lax
+from jax.experimental import pallas as pl
+from jax.experimental.pallas import tpu as pltpu
 from jax.sharding import PartitionSpec as P
+
+MIB = 2**20
+VMEM = pl.BlockSpec(memory_space=pltpu.VMEM)
+HBM = pl.BlockSpec(memory_space=pltpu.HBM)
 
 
 def passed_along(x, axis, by):
@@ -10,7 +18,228 @@
     return lax.ppermute(x, axis, pairs)
 
 
-def per_device(held, fresh, routes, norm_gain, router, w_gate, w_up, w_down):
+def swapped(x, k):
+    length = lax.axis_size("expert")
+    return lax.ppermute(x, "expert", [(i, i ^ k) for i in range(length)])
+
+
+def slot_hits(routes, experts, capacity, route):
+    tokens = routes.shape[1]
+    me = lax.axis_index("expert")
+    ids = lax.broadcasted_iota(jnp.int32, (experts, tokens), 0) ^ me
+    first = (routes[0:1] == ids).astype(jnp.float32)
+    second = (routes[1:2] == ids).astype(jnp.float32)
+    hits = first + second
+    before = lax.broadcasted_iota(jnp.int32, (tokens, tokens), 0) < lax.broadcasted_iota(
+        jnp.int32, (tokens, tokens), 1
+    )
+    rank = jnp.dot(hits, before.astype(jnp.float32), preferred_element_type=jnp.float32)
+    slots = lax.broadcasted_iota(jnp.int32, (experts, capacity, tokens), 1).astype(jnp.float32)
+    chosen = {0: first, 1: second, None: hits}[route]
+    placed = jnp.where(slots == rank[:, None, :], chosen[:, None, :], 0.0)
+    return placed.reshape(experts * capacity, tokens)
+
+
+def normed_rows(values, gain):
+    mean_square = jnp.mean(values * values, axis=-1, keepdims=True)
+    return (values * lax.rsqrt(mean_square + 1e-05) * gain).astype(jnp.bfloat16)
+
+
+def prepare_kernel(
+    experts, capacity, fresh, routes, gain, placing, fresh_here, routes_here, gain_here, sems
+):
+    pairs = ((routes, routes_here), (fresh, fresh_here), (gain, gain_here))
+    copies = [pltpu.make_async_copy(a, b, sems.at[i]) for i, (a, b) in enumerate(pairs)]
+    for copy in copies:
+        copy.start()
+    copies[0].wait()
+    placing[...] = slot_hits(routes_here[...], experts, capacity, None).astype(jnp.bfloat16)
+    copies[1].wait()
+    copies[2].wait()
+
+
+def pack_kernel(received, fresh, gain, placing, inputs, normed, *blocks):
+    section = lax.axis_index("pipe")
+    tile = jnp.where(section == 0, fresh[...], received[...])
+    inputs[...] = tile
+    rows = normed_rows(tile.astype(jnp.float32), gain[...])
+    normed[...] = rows
+    capacity = blocks[0].shape[0]
+    packed = jnp.dot(placing[...], rows, preferred_element_type=jnp.float32).astype(jnp.bfloat16)
+    for k, block in enumerate(blocks):
+        block[...] = packed[k * capacity : (k + 1) * capacity]
+
+
+def weigh_kernel(normed, router, routes, weights):
+    experts = router.shape[0]
+    capacity = weights.shape[1] // experts
+    logits = lax.dot_general(
+        router[...], normed[...], (((1,), (1,)), ((), ())), preferred_element_type=jnp.float32
+    )
+    tokens = logits.shape[1]
+    ids = lax.broadcasted_iota(jnp.int32, (experts, tokens), 0)
+    picked = [
+        jnp.sum(jnp.where(routes[r : r + 1, :] == ids, logits, 0.0), axis=0, keepdims=True)
+        for r in range(2)
+    ]
+    total = 0.0
+    for r in range(2):
+        share = jax.nn.sigmoid(picked[r] - picked[1 - r])
+        total += slot_hits(routes[...], experts, capacity, r) * share
+    for term in range(3):
+        part = total.astype(jnp.bfloat16)
+        weights[term] = part
+        total = total - part.astype(jnp.float32)
+
+
+def ffn_kernel(chunk, ring, *refs):
+    count = (len(refs) - 7) // 2
+    blocks, (gate, up, down), outs = refs[:count], refs[count : count + 3], refs[count + 3 : 2 * count + 3]
+    rows, total, slots, sems = refs[2 * count + 3 :][:4]
+    capacity = blocks[0].shape[0]
+    piece = slots.shape[1]
+    per_chunk = chunk // piece
+    pieces = down.shape[0] // piece
+
+    def fetch(i):
+        return pltpu.make_async_copy(
+            down.at[pl.ds(i * piece, piece)], slots.at[lax.rem(i, ring)], sems.at[lax.rem(i, ring)]
+        )
+
+    for i in range(ring):
+        fetch(i).start()
+    for k in range(count):
+        rows[k * capacity : (k + 1) * capacity, :] = blocks[k][...]
+    total[...] = jnp.zeros_like(total)
+
+    def step(c, _):
+        columns = pl.ds(pl.multiple_of(c * chunk, chunk), chunk)
+        x = rows[...]
+        gate_proj = jnp.dot(x, gate[:, columns], preferred_element_type=jnp.float32)
+        up_proj = jnp.dot(x, up[:, columns], preferred_element_type=jnp.float32)
+        hidden = (jax.nn.silu(gate_proj) * up_proj).astype(jnp.bfloat16)
+        for j in range(per_chunk):
+            i = c * per_chunk + j
+            fetch(i).wait()
+        parts = [
+            jnp.dot(
+                hidden[:, j * piece : (j + 1) * piece],
+                slots[lax.rem(c * per_chunk + j, ring)],
+                preferred_element_type=jnp.float32,
+            )
+            for j in range(per_chunk)
+        ]
+        total[...] += functools.reduce(lambda a, b: a + b, parts)
+        for j in range(per_chunk):
+            i = c * per_chunk + j
+
+            @pl.when(i + ring < pieces)
+            def _():
+                fetch(i + ring).start()
+
+        return 0
+
+    lax.fori_loop(0, down.shape[0] // chunk, step, 0)
+    for k in range(count):
+        outs[k][...] = total[k * capacity : (k + 1) * capacity, :].astype(jnp.bfloat16)
+
+
+def combine_kernel(order, inputs, weights, *refs):
+    blocks, out, back = refs[:-2], refs[-2], refs[-1]
+    capacity = blocks[0].shape[0]
+    for k, block in zip(order, blocks):
+        back[k * capacity : (k + 1) * capacity, :] = block[...]
+    branch = 0.0
+    for term in range(3):
+        branch += lax.dot_general(
+            weights[term], back[...], (((0,), (0,)), ((), ())), preferred_element_type=jnp.float32
+        )
+    out[...] = (inputs[...].astype(jnp.float32) + branch).astype(jnp.bfloat16)
+
+
+def in_vmem(x):
+    return pltpu.with_memory_space_constraint(x, pltpu.VMEM)
+
+
+def in_hbm(x):
+    return pltpu.with_memory_space_constraint(x, pltpu.HBM)
+
+
+def call(kernel, out_shape, in_specs, flops=0, moved=0, limit=2 * MIB, scratch=()):
+    return pl.pallas_call(
+        kernel,
+        out_shape=out_shape,
+        in_specs=in_specs,
+        out_specs=jax.tree.map(lambda _: VMEM, out_shape),
+        scratch_shapes=scratch,
+        compiler_params=pltpu.CompilerParams(vmem_limit_bytes=limit),
+        cost_estimate=pl.CostEstimate(flops=flops, bytes_accessed=moved, transcendentals=0),
+    )
+
+
+def one_expert_each(held, fresh, routes, norm_gain, router, w_gate, w_up, w_down):
+    tokens, width = fresh.shape
+    experts = router.shape[2]
+    capacity = tokens // 2
+    slots = experts * capacity
+    hidden_units = w_gate.shape[3]
+    bf16 = jnp.bfloat16
+    chosen = jnp.transpose(routes[0])
+    router_rows = jnp.transpose(router[0])
+    received = passed_along(held[0], "pipe", 1)
+    placing, fresh_here, routes_here, gain_here = call(
+        functools.partial(prepare_kernel, experts, capacity),
+        [
+            pltpu.VMEM((slots, tokens), bf16),
+            pltpu.VMEM(fresh.shape, bf16),
+            pltpu.VMEM(chosen.shape, jnp.int32),
+            pltpu.VMEM(norm_gain.shape, jnp.float32),
+        ],
+        [HBM] * 3,
+        flops=10**6,
+        moved=10**6,
+        scratch=[pltpu.SemaphoreType.DMA((3,))],
+    )(*map(in_hbm, (fresh, chosen, norm_gain)))
+    tile = pltpu.VMEM((tokens, width), bf16)
+    block = pltpu.VMEM((capacity, width), bf16)
+    inputs, normed, *packed = call(
+        pack_kernel, [tile, tile] + [block] * experts, [VMEM] * 4, flops=30 * 10**9, moved=10**6
+    )(*map(in_vmem, (received, fresh_here, gain_here, placing)))
+    order = range(experts - 1, -1, -1)
+    arrived = [swapped(packed[k], k) if k else packed[k] for k in order]
+    weights = call(
+        weigh_kernel, pltpu.VMEM((3, slots, tokens), bf16), [VMEM] * 3, flops=10**6, moved=10**5
+    )(in_vmem(normed), router_rows, in_vmem(routes_here))
+    weights_in = [in_vmem(w_gate[0, 0]), in_vmem(w_up[0, 0]), in_hbm(w_down[0, 0])]
+    piece, ring, chunk = 256, 3, 512
+    results = call(
+        functools.partial(ffn_kernel, chunk, ring),
+        [block] * experts,
+        [VMEM] * (experts + 2) + [HBM],
+        flops=6 * slots * width * hidden_units,
+        moved=6 * width * hidden_units,
+        limit=6 * MIB,
+        scratch=[
+            pltpu.VMEM((slots, width), bf16),
+            pltpu.VMEM((slots, width), jnp.float32),
+            pltpu.VMEM((ring, piece, width), bf16),
+            pltpu.SemaphoreType.DMA((ring,)),
+        ],
+    )(*map(in_vmem, arrived), *weights_in)
+    returned = [swapped(result, k) if k else result for result, k in zip(results, order)]
+    out = call(
+        functools.partial(combine_kernel, order),
+        jax.ShapeDtypeStruct((tokens, width), bf16),
+        [VMEM] * (experts + 2),
+        flops=10**8,
+        moved=10**6,
+        limit=4 * MIB,
+        scratch=[pltpu.VMEM((slots, width), bf16)],
+    )(*map(in_vmem, (inputs, weights, *returned)))
+    return out[None]
+
+
+def shared_experts(held, fresh, routes, norm_gain, router, w_gate, w_up, w_down):
     tok_rows = fresh.shape[0]
     model_width = fresh.shape[1]
     experts = router.shape[2]
@@ -21,8 +250,7 @@
     section_index = lax.axis_index("pipe")
     inputs = jnp.where(section_index == 0, fresh, received)
     values = inputs.astype(jnp.float32)
-    mean_square = jnp.mean(values * values, axis=-1, keepdims=True)
-    normed = (values * lax.rsqrt(mean_square + 1e-05) * norm_gain[0]).astype(jnp.bfloat16)
+    normed = normed_rows(values, norm_gain[0])
     logits = jnp.dot(normed, router[0], preferred_element_type=jnp.float32)
     chosen = routes[0]
     expert_ids = jnp.arange(experts, dtype=jnp.int32)
@@ -77,6 +305,12 @@
     return section_out[None]
 
 
+def per_device(*args):
+    experts = args[4].shape[2]
+    alone = lax.axis_size("expert") == experts and experts & (experts - 1) == 0
+    return (one_expert_each if alone else shared_experts)(*args)
+
+
 def solution(mesh):
     in_specs = (
         P("pipe", "expert", None),

time: 86.9 us -> 62.7 us (0.72)
  the two profiles are of different devices: /device:TPU:0 before, /device:TPU:1 now
where the time goes in v1:
time: 62.7 us; the launch traced here: 61.8 us
  starting transfers between devices  26.5 us (42%)
  Pallas kernels  24.3 us (39%)
  waiting for transfers between devices  8.21 us (13%)
  local copies, waits for them, and re-layouts  2.74 us (4%)
    ppermute x14, starting transfers between devices, swapped(): return lax.ppermute(x, 'expert', [(i, i ^ k) for i in range(length)])  22 us
    pallas_call x1, Pallas kernels, one_expert_each(): call(functools.partial(ffn_kernel, chunk, ring), [block] * experts, [VMEM...  21.7 us
    ppermute x14, waiting for transfers between devices, swapped(): return lax.ppermute(x, 'expert', [(i, i ^ k) for i in range(length)])  6.93 us
    ppermute x1, starting transfers between devices, passed_along(): return lax.ppermute(x, axis, pairs)  4.5 us
    unnamed x6, local copies, waits for them, and re-layouts  2.74 us
    ppermute x1, waiting for transfers between devices, passed_along(): return lax.ppermute(x, axis, pairs)  1.28 us
  transfers between devices with their start and end apart: 15, of which 7 were waited for; matrix products, arithmetic and copies ran while one was open for 0% of the time, Pallas kernels for 2%

profile of v1, /device:TPU:1, one launch (start us, length us, event | category | flops | bytes accessed | tf_op | source)
XLA Modules:
  0.0 61.8 jit_solution(17502459294095562692)
XLA Ops:
  0.0 4.5 %collective-permute-start = (bf16[32,2048]{1,0:T(8,128)(2,1)}, bf16[32,2048]{1,0:T(8,128)(2,1)S(1)}, u32[]{:S(2)}, u32[]{:S(2)}) collective-permute-start(bf16[32,2048]{1,0:T(8,128)(2,1)} %bitcast.16), channel_id=1, source_target_pairs={{0,8},{8,16},{16,24},{1,9},{9,17},{17,25},{2,10},{10,18},{18,26},{... | collective-permute-start | bytes 393224 | tf_op jit(solution)/shard_map/ppermute | solution.py:18
  4.5 0.9 %shard_map.82 = (bf16[128,32]{1,0:T(8,128)(2,1)S(1)}, bf16[32,2048]{1,0:T(8,128)(2,1)S(1)}, s32[2,32]{1,0:T(2,128)S(1)}, f32[1,2048]{1,0:T(1,128)S(1)}) custom-call(bf16[32,2048]{1,0:T(8,128)(2,1)} %fresh.1, s32[2,32]{1,0:T(2,128)} %bitcast.15, f32[1,2048]{1,0:T(1,128)} %gain.1), custom_call_target="tpu_custom_call" | custom-call | flops 1000000 | bytes 1000000 | tf_op jit(solution)/shard_map/pallas_call | solution.py:190
  5.5 1.3 %collective-permute-done.received = bf16[32,2048]{1,0:T(8,128)(2,1)S(1)} collective-permute-done((bf16[32,2048]{1,0:T(8,128)(2,1)}, bf16[32,2048]{1,0:T(8,128)(2,1)S(1)}, u32[]{:S(2)}, u32[]{:S(2)}) %collective-permute-start) | collective-permute-done | bytes 131104 | tf_op jit(solution)/shard_map/ppermute | solution.py:18
  6.7 0.0 copy-start
  6.7 0.0 copy-start.1
  6.8 0.4 shard_map.83
  7.2 4.3 %collective-permute-start.1 = (bf16[16,2048]{1,0:T(8,128)(2,1)S(1)}, bf16[16,2048]{1,0:T(8,128)(2,1)S(1)}, u32[]{:S(2)}, u32[]{:S(2)}) collective-permute-start(bf16[16,2048]{1,0:T(8,128)(2,1)S(1)} %get-tuple-element.33), channel_id=1, source_target_pairs={{0,7},{1,6},{2,5},{3,4},{4,3},{5,2},{6,1},{7,0},{8,15},{9,14},{10,... | collective-permute-start | bytes 196616 | tf_op jit(solution)/shard_map/ppermute | solution.py:23
  11.5 0.0 collective-permute-start.2
  11.5 0.4 collective-permute-start.3
  11.9 2.0 %collective-permute-start.4 = (bf16[16,2048]{1,0:T(8,128)(2,1)S(1)}, bf16[16,2048]{1,0:T(8,128)(2,1)S(1)}, u32[]{:S(2)}, u32[]{:S(2)}) collective-permute-start(bf16[16,2048]{1,0:T(8,128)(2,1)S(1)} %get-tuple-element.36), channel_id=1, source_target_pairs={{0,4},{1,5},{2,6},{3,7},{4,0},{5,1},{6,2},{7,3},{8,12},{9,13},{10,... | collective-permute-start | bytes 196616 | tf_op jit(solution)/shard_map/ppermute | solution.py:23
  13.9 2.0 %collective-permute-start.5 = (bf16[16,2048]{1,0:T(8,128)(2,1)S(1)}, bf16[16,2048]{1,0:T(8,128)(2,1)S(1)}, u32[]{:S(2)}, u32[]{:S(2)}) collective-permute-start(bf16[16,2048]{1,0:T(8,128)(2,1)S(1)} %get-tuple-element.37), channel_id=1, source_target_pairs={{0,3},{1,2},{2,1},{3,0},{4,7},{5,6},{6,5},{7,4},{8,11},{9,10},{10,... | collective-permute-start | bytes 196616 | tf_op jit(solution)/shard_map/ppermute | solution.py:23
  16.0 0.0 collective-permute-done.1.refs_0_
  16.0 2.2 %collective-permute-start.6 = (bf16[16,2048]{1,0:T(8,128)(2,1)S(1)}, bf16[16,2048]{1,0:T(8,128)(2,1)S(1)}, u32[]{:S(2)}, u32[]{:S(2)}) collective-permute-start(bf16[16,2048]{1,0:T(8,128)(2,1)S(1)} %get-tuple-element.38), channel_id=1, source_target_pairs={{0,2},{1,3},{2,0},{3,1},{4,6},{5,7},{6,4},{7,5},{8,10},{9,11},{10,... | collective-permute-start | bytes 196616 | tf_op jit(solution)/shard_map/ppermute | solution.py:23
  18.2 0.0 collective-permute-done.2.refs_1_
  18.2 0.0 collective-permute-start.7
  18.2 1.2 %collective-permute-done.3.refs_2_ = bf16[16,2048]{1,0:T(8,128)(2,1)S(1)} collective-permute-done((bf16[16,2048]{1,0:T(8,128)(2,1)S(1)}, bf16[16,2048]{1,0:T(8,128)(2,1)S(1)}, u32[]{:S(2)}, u32[]{:S(2)}) %collective-permute-start.3) | collective-permute-done | bytes 65568 | tf_op jit(solution)/shard_map/ppermute | solution.py:23
  19.4 1.9 %collective-permute-done.4.refs_3_ = bf16[16,2048]{1,0:T(8,128)(2,1)S(1)} collective-permute-done((bf16[16,2048]{1,0:T(8,128)(2,1)S(1)}, bf16[16,2048]{1,0:T(8,128)(2,1)S(1)}, u32[]{:S(2)}, u32[]{:S(2)}) %collective-permute-start.4) | collective-permute-done | bytes 65568 | tf_op jit(solution)/shard_map/ppermute | solution.py:23
  21.3 0.0 collective-permute-done.5.refs_4_
  21.3 0.5 collective-permute-done.6.refs_5_
  21.7 0.0 collective-permute-done.7.refs_6_
  21.7 0.0 copy-done
  21.7 2.7 %copy-done.1 = bf16[1,1,2048,7168]{3,2,1,0:T(8,128)(2,1)S(1)} copy-done((bf16[1,1,2048,7168]{3,2,1,0:T(8,128)(2,1)S(1)}, bf16[1,1,2048,7168]{3,2,1,0:T(8,128)(2,1)}, u32[]{:S(2)}) %copy-start.1) | copy-done | bytes 29360152
  24.5 0.0 copy-start.2
  24.5 21.7 %shard_map.85 = (bf16[16,2048]{1,0:T(8,128)(2,1)S(1)}, bf16[16,2048]{1,0:T(8,128)(2,1)S(1)}, bf16[16,2048]{1,0:T(8,128)(2,1)S(1)}, bf16[16,2048]{1,0:T(8,128)(2,...) custom-call(bf16[16,2048]{1,0:T(8,128)(2,1)S(1)} %collective-permute, ...), custom_call_target="tpu_custom_call" | custom-call | flops 11274289152 | bytes 88080384 | tf_op jit(solution)/shard_map/pallas_call | solution.py:215
  46.2 4.3 %collective-permute-start.8 = (bf16[16,2048]{1,0:T(8,128)(2,1)S(1)}, bf16[16,2048]{1,0:T(8,128)(2,1)S(1)}, u32[]{:S(2)}, u32[]{:S(2)}) collective-permute-start(bf16[16,2048]{1,0:T(8,128)(2,1)S(1)} %get-tuple-element.41), channel_id=1, source_target_pairs={{0,7},{1,6},{2,5},{3,4},{4,3},{5,2},{6,1},{7,0},{8,15},{9,14},{10,... | collective-permute-start | bytes 196616 | tf_op jit(solution)/shard_map/ppermute | solution.py:23
  50.6 0.0 collective-permute-start.9
  50.6 0.4 collective-permute-start.10
  50.9 2.0 %collective-permute-start.11 = (bf16[16,2048]{1,0:T(8,128)(2,1)S(1)}, bf16[16,2048]{1,0:T(8,128)(2,1)S(1)}, u32[]{:S(2)}, u32[]{:S(2)}) collective-permute-start(bf16[16,2048]{1,0:T(8,128)(2,1)S(1)} %get-tuple-element.44), channel_id=1, source_target_pairs={{0,4},{1,5},{2,6},{3,7},{4,0},{5,1},{6,2},{7,3},{8,12},{9,13},{10,... | collective-permute-start | bytes 196616 | tf_op jit(solution)/shard_map/ppermute | solution.py:23
  53.0 2.0 %collective-permute-start.12 = (bf16[16,2048]{1,0:T(8,128)(2,1)S(1)}, bf16[16,2048]{1,0:T(8,128)(2,1)S(1)}, u32[]{:S(2)}, u32[]{:S(2)}) collective-permute-start(bf16[16,2048]{1,0:T(8,128)(2,1)S(1)} %get-tuple-element.45), channel_id=1, source_target_pairs={{0,3},{1,2},{2,1},{3,0},{4,7},{5,6},{6,5},{7,4},{8,11},{9,10},{10,... | collective-permute-start | bytes 196616 | tf_op jit(solution)/shard_map/ppermute | solution.py:23
  55.0 0.0 collective-permute-done.8.refs_0_
  55.0 2.2 %collective-permute-start.13 = (bf16[16,2048]{1,0:T(8,128)(2,1)S(1)}, bf16[16,2048]{1,0:T(8,128)(2,1)S(1)}, u32[]{:S(2)}, u32[]{:S(2)}) collective-permute-start(bf16[16,2048]{1,0:T(8,128)(2,1)S(1)} %get-tuple-element.46), channel_id=1, source_target_pairs={{0,2},{1,3},{2,0},{3,1},{4,6},{5,7},{6,4},{7,5},{8,10},{9,11},{10,... | collective-permute-start | bytes 196616 | tf_op jit(solution)/shard_map/ppermute | solution.py:23
  57.2 0.0 collective-permute-done.9.refs_1_
  57.2 0.0 collective-permute-start.14
  57.2 0.0 copy-done.2
  57.2 0.2 shard_map.84.weights
  57.4 1.0 %collective-permute-done.10.refs_2_ = bf16[16,2048]{1,0:T(8,128)(2,1)S(1)} collective-permute-done((bf16[16,2048]{1,0:T(8,128)(2,1)S(1)}, bf16[16,2048]{1,0:T(8,128)(2,1)S(1)}, u32[]{:S(2)}, u32[]{:S(2)}) %collective-permute-start.10) | collective-permute-done | bytes 65568 | tf_op jit(solution)/shard_map/ppermute | solution.py:23
  58.4 1.9 %collective-permute-done.11.refs_3_ = bf16[16,2048]{1,0:T(8,128)(2,1)S(1)} collective-permute-done((bf16[16,2048]{1,0:T(8,128)(2,1)S(1)}, bf16[16,2048]{1,0:T(8,128)(2,1)S(1)}, u32[]{:S(2)}, u32[]{:S(2)}) %collective-permute-start.11) | collective-permute-done | bytes 65568 | tf_op jit(solution)/shard_map/ppermute | solution.py:23
  60.3 0.0 collective-permute-done.12.refs_4_
  60.3 0.5 collective-permute-done.13.refs_5_
  60.8 0.0 collective-permute-done.14.refs_6_
  60.8 1.0 %shard_map.86 = bf16[32,2048]{1,0:T(8,128)(2,1)} custom-call(bf16[32,2048]{1,0:T(8,128)(2,1)S(1)} %get-tuple-element.30.inputs, bf16[3,128,32]{2,1,0:T(8,128)(2,1)S(1)} %shard_map.84.weights, bf16[16,2048]{1,0:T(8,128)(2,1)S(1)} %collective-permute-done.8.refs_0_, bf16[16,2048]{1,0:T(8,128)(2,1)S(1)} %collective-permute-done.9.refs_1_, ...), custom_call_target="tpu_custom_call" | custom-call | flops 100000000 | bytes 1000000 | tf_op jit(solution)/shard_map/pallas_call | solution.py:230
Async XLA Ops:
  0.0 6.7 %collective-permute-start = (bf16[32,2048]{1,0:T(8,128)(2,1)}, bf16[32,2048]{1,0:T(8,128)(2,1)S(1)}, u32[]{:S(2)}, u32[]{:S(2)}) collective-permute-start(bf16[32,2048]{1,0:T(8,128)(2,1)} %bitcast.16), channel_id=1, source_target_pairs={{0,8},{8,16},{16,24},{1,9},{9,17},{17,25},{2,10},{10,18},{18,26},{... | collective-permute-start | bytes 393224 | tf_op jit(solution)/shard_map/ppermute | solution.py:18
  6.7 15.0 %copy-start = (bf16[1,1,2048,7168]{3,2,1,0:T(8,128)(2,1)S(1)}, bf16[1,1,2048,7168]{3,2,1,0:T(8,128)(2,1)}, u32[]{:S(2)}) copy-start(bf16[1,1,2048,7168]{3,2,1,0:T(8,128)(2,1)} %param.13) | copy-start | bytes 88080384
  6.7 17.7 %copy-start.1 = (bf16[1,1,2048,7168]{3,2,1,0:T(8,128)(2,1)S(1)}, bf16[1,1,2048,7168]{3,2,1,0:T(8,128)(2,1)}, u32[]{:S(2)}) copy-start(bf16[1,1,2048,7168]{3,2,1,0:T(8,128)(2,1)} %param.14) | copy-start | bytes 88080384
  7.2 8.8 %collective-permute-start.1 = (bf16[16,2048]{1,0:T(8,128)(2,1)S(1)}, bf16[16,2048]{1,0:T(8,128)(2,1)S(1)}, u32[]{:S(2)}, u32[]{:S(2)}) collective-permute-start(bf16[16,2048]{1,0:T(8,128)(2,1)S(1)} %get-tuple-element.33), channel_id=1, source_target_pairs={{0,7},{1,6},{2,5},{3,4},{4,3},{5,2},{6,1},{7,0},{8,15},{9,14},{10,... | collective-permute-start | bytes 196616 | tf_op jit(solution)/shard_map/ppermute | solution.py:23
  11.5 6.7 %collective-permute-start.2 = (bf16[16,2048]{1,0:T(8,128)(2,1)S(1)}, bf16[16,2048]{1,0:T(8,128)(2,1)S(1)}, u32[]{:S(2)}, u32[]{:S(2)}) collective-permute-start(bf16[16,2048]{1,0:T(8,128)(2,1)S(1)} %get-tuple-element.34), channel_id=1, source_target_pairs={{0,6},{1,7},{2,4},{3,5},{4,2},{5,3},{6,0},{7,1},{8,14},{9,15},{10,... | collective-permute-start | bytes 196616 | tf_op jit(solution)/shard_map/ppermute | solution.py:23
  11.5 7.9 %collective-permute-start.3 = (bf16[16,2048]{1,0:T(8,128)(2,1)S(1)}, bf16[16,2048]{1,0:T(8,128)(2,1)S(1)}, u32[]{:S(2)}, u32[]{:S(2)}) collective-permute-start(bf16[16,2048]{1,0:T(8,128)(2,1)S(1)} %get-tuple-element.35), channel_id=1, source_target_pairs={{0,5},{1,4},{2,7},{3,6},{4,1},{5,0},{6,3},{7,2},{8,13},{9,12},{10,... | collective-permute-start | bytes 196616 | tf_op jit(solution)/shard_map/ppermute | solution.py:23
  11.9 9.4 %collective-permute-start.4 = (bf16[16,2048]{1,0:T(8,128)(2,1)S(1)}, bf16[16,2048]{1,0:T(8,128)(2,1)S(1)}, u32[]{:S(2)}, u32[]{:S(2)}) collective-permute-start(bf16[16,2048]{1,0:T(8,128)(2,1)S(1)} %get-tuple-element.36), channel_id=1, source_target_pairs={{0,4},{1,5},{2,6},{3,7},{4,0},{5,1},{6,2},{7,3},{8,12},{9,13},{10,... | collective-permute-start | bytes 196616 | tf_op jit(solution)/shard_map/ppermute | solution.py:23
  13.9 7.3 %collective-permute-start.5 = (bf16[16,2048]{1,0:T(8,128)(2,1)S(1)}, bf16[16,2048]{1,0:T(8,128)(2,1)S(1)}, u32[]{:S(2)}, u32[]{:S(2)}) collective-permute-start(bf16[16,2048]{1,0:T(8,128)(2,1)S(1)} %get-tuple-element.37), channel_id=1, source_target_pairs={{0,3},{1,2},{2,1},{3,0},{4,7},{5,6},{6,5},{7,4},{8,11},{9,10},{10,... | collective-permute-start | bytes 196616 | tf_op jit(solution)/shard_map/ppermute | solution.py:23
  16.0 5.8 %collective-permute-start.6 = (bf16[16,2048]{1,0:T(8,128)(2,1)S(1)}, bf16[16,2048]{1,0:T(8,128)(2,1)S(1)}, u32[]{:S(2)}, u32[]{:S(2)}) collective-permute-start(bf16[16,2048]{1,0:T(8,128)(2,1)S(1)} %get-tuple-element.38), channel_id=1, source_target_pairs={{0,2},{1,3},{2,0},{3,1},{4,6},{5,7},{6,4},{7,5},{8,10},{9,11},{10,... | collective-permute-start | bytes 196616 | tf_op jit(solution)/shard_map/ppermute | solution.py:23
  18.2 3.6 %collective-permute-start.7 = (bf16[16,2048]{1,0:T(8,128)(2,1)S(1)}, bf16[16,2048]{1,0:T(8,128)(2,1)S(1)}, u32[]{:S(2)}, u32[]{:S(2)}) collective-permute-start(bf16[16,2048]{1,0:T(8,128)(2,1)S(1)} %get-tuple-element.39), channel_id=1, source_target_pairs={{0,1},{1,0},{2,3},{3,2},{4,5},{5,4},{6,7},{7,6},{8,9},{9,8},{10,11... | collective-permute-start | bytes 196616 | tf_op jit(solution)/shard_map/ppermute | solution.py:23
  24.5 32.8 %copy-start.2 = (bf16[1,2048,8]{1,2,0:T(8,128)(2,1)S(1)}, bf16[1,2048,8]{1,2,0:T(8,128)(2,1)}, u32[]{:S(2)}) copy-start(bf16[1,2048,8]{1,2,0:T(8,128)(2,1)} %param.12) | copy-start | bytes 98308
  46.2 8.8 %collective-permute-start.8 = (bf16[16,2048]{1,0:T(8,128)(2,1)S(1)}, bf16[16,2048]{1,0:T(8,128)(2,1)S(1)}, u32[]{:S(2)}, u32[]{:S(2)}) collective-permute-start(bf16[16,2048]{1,0:T(8,128)(2,1)S(1)} %get-tuple-element.41), channel_id=1, source_target_pairs={{0,7},{1,6},{2,5},{3,4},{4,3},{5,2},{6,1},{7,0},{8,15},{9,14},{10,... | collective-permute-start | bytes 196616 | tf_op jit(solution)/shard_map/ppermute | solution.py:23
  50.6 6.7 %collective-permute-start.9 = (bf16[16,2048]{1,0:T(8,128)(2,1)S(1)}, bf16[16,2048]{1,0:T(8,128)(2,1)S(1)}, u32[]{:S(2)}, u32[]{:S(2)}) collective-permute-start(bf16[16,2048]{1,0:T(8,128)(2,1)S(1)} %get-tuple-element.42), channel_id=1, source_target_pairs={{0,6},{1,7},{2,4},{3,5},{4,2},{5,3},{6,0},{7,1},{8,14},{9,15},{10,... | collective-permute-start | bytes 196616 | tf_op jit(solution)/shard_map/ppermute | solution.py:23
  50.6 7.9 %collective-permute-start.10 = (bf16[16,2048]{1,0:T(8,128)(2,1)S(1)}, bf16[16,2048]{1,0:T(8,128)(2,1)S(1)}, u32[]{:S(2)}, u32[]{:S(2)}) collective-permute-start(bf16[16,2048]{1,0:T(8,128)(2,1)S(1)} %get-tuple-element.43), channel_id=1, source_target_pairs={{0,5},{1,4},{2,7},{3,6},{4,1},{5,0},{6,3},{7,2},{8,13},{9,12},{10,... | collective-permute-start | bytes 196616 | tf_op jit(solution)/shard_map/ppermute | solution.py:23
  50.9 9.4 %collective-permute-start.11 = (bf16[16,2048]{1,0:T(8,128)(2,1)S(1)}, bf16[16,2048]{1,0:T(8,128)(2,1)S(1)}, u32[]{:S(2)}, u32[]{:S(2)}) collective-permute-start(bf16[16,2048]{1,0:T(8,128)(2,1)S(1)} %get-tuple-element.44), channel_id=1, source_target_pairs={{0,4},{1,5},{2,6},{3,7},{4,0},{5,1},{6,2},{7,3},{8,12},{9,13},{10,... | collective-permute-start | bytes 196616 | tf_op jit(solution)/shard_map/ppermute | solution.py:23
  53.0 7.3 %collective-permute-start.12 = (bf16[16,2048]{1,0:T(8,128)(2,1)S(1)}, bf16[16,2048]{1,0:T(8,128)(2,1)S(1)}, u32[]{:S(2)}, u32[]{:S(2)}) collective-permute-start(bf16[16,2048]{1,0:T(8,128)(2,1)S(1)} %get-tuple-element.45), channel_id=1, source_target_pairs={{0,3},{1,2},{2,1},{3,0},{4,7},{5,6},{6,5},{7,4},{8,11},{9,10},{10,... | collective-permute-start | bytes 196616 | tf_op jit(solution)/shard_map/ppermute | solution.py:23
  55.0 5.8 %collective-permute-start.13 = (bf16[16,2048]{1,0:T(8,128)(2,1)S(1)}, bf16[16,2048]{1,0:T(8,128)(2,1)S(1)}, u32[]{:S(2)}, u32[]{:S(2)}) collective-permute-start(bf16[16,2048]{1,0:T(8,128)(2,1)S(1)} %get-tuple-element.46), channel_id=1, source_target_pairs={{0,2},{1,3},{2,0},{3,1},{4,6},{5,7},{6,4},{7,5},{8,10},{9,11},{10,... | collective-permute-start | bytes 196616 | tf_op jit(solution)/shard_map/ppermute | solution.py:23
  57.2 3.6 %collective-permute-start.14 = (bf16[16,2048]{1,0:T(8,128)(2,1)S(1)}, bf16[16,2048]{1,0:T(8,128)(2,1)S(1)}, u32[]{:S(2)}, u32[]{:S(2)}) collective-permute-start(bf16[16,2048]{1,0:T(8,128)(2,1)S(1)} %get-tuple-element.47), channel_id=1, source_target_pairs={{0,1},{1,0},{2,3},{3,2},{4,5},{5,4},{6,7},{7,6},{8,9},{9,8},{10,11... | collective-permute-start | bytes 196616 | tf_op jit(solution)/shard_map/ppermute | solution.py:23

commit v2 on v1

--- a/solution.py
+++ b/solution.py
@@ -8,6 +8,9 @@
 from jax.sharding import PartitionSpec as P
 
 MIB = 2**20
+CHUNK, BAND = 1024, 512
+HEAD = 4096
+TERMS = 3
 VMEM = pl.BlockSpec(memory_space=pltpu.VMEM)
 HBM = pl.BlockSpec(memory_space=pltpu.HBM)
 
@@ -54,8 +57,8 @@
         copy.start()
     copies[0].wait()
     placing[...] = slot_hits(routes_here[...], experts, capacity, None).astype(jnp.bfloat16)
-    copies[1].wait()
-    copies[2].wait()
+    for copy in copies[1:]:
+        copy.wait()
 
 
 def pack_kernel(received, fresh, gain, placing, inputs, normed, *blocks):
@@ -70,9 +73,11 @@
         block[...] = packed[k * capacity : (k + 1) * capacity]
 
 
-def weigh_kernel(normed, router, routes, weights):
+def weigh_kernel(head, normed, router, routes, up, weights, up_here, sem):
+    fetch = pltpu.make_async_copy(up.at[:, :head], up_here.at[:, :head], sem)
+    fetch.start()
     experts = router.shape[0]
-    capacity = weights.shape[1] // experts
+    slots = weights.shape[1]
     logits = lax.dot_general(
         router[...], normed[...], (((1,), (1,)), ((), ())), preferred_element_type=jnp.float32
     )
@@ -85,63 +90,79 @@
     total = 0.0
     for r in range(2):
         share = jax.nn.sigmoid(picked[r] - picked[1 - r])
-        total += slot_hits(routes[...], experts, capacity, r) * share
-    for term in range(3):
+        total += slot_hits(routes[...], experts, slots // experts, r) * share
+    diagonal = lax.broadcasted_iota(jnp.int32, (slots, slots), 0) == lax.broadcasted_iota(
+        jnp.int32, (slots, slots), 1
+    )
+    for term in range(TERMS):
         part = total.astype(jnp.bfloat16)
-        weights[term] = part
+        weights[term * tokens : (term + 1) * tokens, :] = lax.dot_general(
+            part,
+            diagonal.astype(jnp.bfloat16),
+            (((0,), (0,)), ((), ())),
+            preferred_element_type=jnp.float32,
+        ).astype(jnp.bfloat16)
         total = total - part.astype(jnp.float32)
-
-
-def ffn_kernel(chunk, ring, *refs):
-    count = (len(refs) - 7) // 2
-    blocks, (gate, up, down), outs = refs[:count], refs[count : count + 3], refs[count + 3 : 2 * count + 3]
-    rows, total, slots, sems = refs[2 * count + 3 :][:4]
+    fetch.wait()
+
+
+def ffn_kernel(count, chunk, band, head, *refs):
+    blocks, (gate, _, up, down) = refs[:count], refs[count : count + 4]
+    outs = refs[count + 4 : 2 * count + 4]
+    spare, rows, hidden, sems, tail_sems = refs[2 * count + 4 :]
     capacity = blocks[0].shape[0]
-    piece = slots.shape[1]
-    per_chunk = chunk // piece
-    pieces = down.shape[0] // piece
-
-    def fetch(i):
-        return pltpu.make_async_copy(
-            down.at[pl.ds(i * piece, piece)], slots.at[lax.rem(i, ring)], sems.at[lax.rem(i, ring)]
-        )
-
-    for i in range(ring):
-        fetch(i).start()
+    width, hidden_units = gate.shape
+    unit = width // 2
+    tall = hidden_units // unit
+
+    def place(u):
+        return pl.ds(u % 2 * unit, unit), pl.ds(u // 2 * band, band)
+
+    def fetch(u):
+        source = down.at[pl.ds(u % tall * unit, unit), pl.ds(u // tall * band, band)]
+        return pltpu.make_async_copy(source, spare.at[place(u)], sems.at[u])
+
+    def fetch_tail(c):
+        columns = pl.ds(pl.multiple_of(c * chunk, chunk), chunk)
+        return pltpu.make_async_copy(up.at[:, columns], spare.at[:, columns], tail_sems.at[c - head // chunk])
+
+    for c in range(head // chunk, hidden_units // chunk):
+        fetch_tail(c).start()
     for k in range(count):
         rows[k * capacity : (k + 1) * capacity, :] = blocks[k][...]
-    total[...] = jnp.zeros_like(total)
-
-    def step(c, _):
+
+    def step(c, fetched):
         columns = pl.ds(pl.multiple_of(c * chunk, chunk), chunk)
         x = rows[...]
+        if not fetched:
+            fetch_tail(c).wait()
         gate_proj = jnp.dot(x, gate[:, columns], preferred_element_type=jnp.float32)
-        up_proj = jnp.dot(x, up[:, columns], preferred_element_type=jnp.float32)
-        hidden = (jax.nn.silu(gate_proj) * up_proj).astype(jnp.bfloat16)
-        for j in range(per_chunk):
-            i = c * per_chunk + j
-            fetch(i).wait()
-        parts = [
-            jnp.dot(
-                hidden[:, j * piece : (j + 1) * piece],
-                slots[lax.rem(c * per_chunk + j, ring)],
+
+        up_proj = jnp.dot(x, spare[:, columns], preferred_element_type=jnp.float32)
+        hidden[:, columns] = (jax.nn.silu(gate_proj) * up_proj).astype(jnp.bfloat16)
+        for j in range(2 * chunk // band):
+            fetch(c * (2 * chunk // band) + j).start()
+
+    pl.loop(0, head // chunk)(lambda c: step(c, True))
+    pl.loop(head // chunk, hidden_units // chunk)(lambda c: step(c, False))
+    for j in range(width // band):
+        total, u = None, j * tall
+        while u < (j + 1) * tall:
+            paired = u % 2 == 0 and u + 1 < (j + 1) * tall
+            for v in range(u, u + 1 + paired):
+                fetch(v).wait()
+            start, columns = u % 2 * unit, place(u)[1]
+            part = jnp.dot(
+                hidden[:, u % tall * unit : (u % tall + 1 + paired) * unit],
+                spare[start : start + (1 + paired) * unit, columns],
                 preferred_element_type=jnp.float32,
             )
-            for j in range(per_chunk)
-        ]
-        total[...] += functools.reduce(lambda a, b: a + b, parts)
-        for j in range(per_chunk):
-            i = c * per_chunk + j
-
-            @pl.when(i + ring < pieces)
-            def _():
-                fetch(i + ring).start()
-
-        return 0
-
-    lax.fori_loop(0, down.shape[0] // chunk, step, 0)
-    for k in range(count):
-        outs[k][...] = total[k * capacity : (k + 1) * capacity, :].astype(jnp.bfloat16)
+            total = part if total is None else total + part
+            u += 1 + paired
+        for k in range(count):
+            outs[k][:, j * band : (j + 1) * band] = total[k * capacity : (k + 1) * capacity].astype(
+                jnp.bfloat16
+            )
 
 
 def combine_kernel(order, inputs, weights, *refs):
@@ -149,12 +170,12 @@
     capacity = blocks[0].shape[0]
     for k, block in zip(order, blocks):
         back[k * capacity : (k + 1) * capacity, :] = block[...]
-    branch = 0.0
-    for term in range(3):
-        branch += lax.dot_general(
-            weights[term], back[...], (((0,), (0,)), ((), ())), preferred_element_type=jnp.float32
-        )
-    out[...] = (inputs[...].astype(jnp.float32) + branch).astype(jnp.bfloat16)
+    terms = jnp.dot(weights[...], back[...], preferred_element_type=jnp.float32)
+    total = inputs[...].astype(jnp.float32)
+    tokens = total.shape[0]
+    for term in range(TERMS):
+        total += terms[term * tokens : (term + 1) * tokens]
+    out[...] = total.astype(jnp.bfloat16)
 
 
 def in_vmem(x):
@@ -165,13 +186,14 @@
     return pltpu.with_memory_space_constraint(x, pltpu.HBM)
 
 
-def call(kernel, out_shape, in_specs, flops=0, moved=0, limit=2 * MIB, scratch=()):
+def call(kernel, out_shape, in_specs, flops=0, moved=0, limit=2 * MIB, scratch=(), aliases={}):
     return pl.pallas_call(
         kernel,
         out_shape=out_shape,
         in_specs=in_specs,
         out_specs=jax.tree.map(lambda _: VMEM, out_shape),
         scratch_shapes=scratch,
+        input_output_aliases=aliases,
         compiler_params=pltpu.CompilerParams(vmem_limit_bytes=limit),
         cost_estimate=pl.CostEstimate(flops=flops, bytes_accessed=moved, transcendentals=0),
     )
@@ -196,36 +218,41 @@
             pltpu.VMEM(norm_gain.shape, jnp.float32),
         ],
         [HBM] * 3,
-        flops=10**6,
+        flops=60 * 10**9,
         moved=10**6,
         scratch=[pltpu.SemaphoreType.DMA((3,))],
     )(*map(in_hbm, (fresh, chosen, norm_gain)))
     tile = pltpu.VMEM((tokens, width), bf16)
     block = pltpu.VMEM((capacity, width), bf16)
     inputs, normed, *packed = call(
-        pack_kernel, [tile, tile] + [block] * experts, [VMEM] * 4, flops=30 * 10**9, moved=10**6
+        pack_kernel, [tile, tile] + [block] * experts, [VMEM] * 4, flops=10**7, moved=10**6
     )(*map(in_vmem, (received, fresh_here, gain_here, placing)))
     order = range(experts - 1, -1, -1)
     arrived = [swapped(packed[k], k) if k else packed[k] for k in order]
-    weights = call(
-        weigh_kernel, pltpu.VMEM((3, slots, tokens), bf16), [VMEM] * 3, flops=10**6, moved=10**5
-    )(in_vmem(normed), router_rows, in_vmem(routes_here))
-    weights_in = [in_vmem(w_gate[0, 0]), in_vmem(w_up[0, 0]), in_hbm(w_down[0, 0])]
-    piece, ring, chunk = 256, 3, 512
-    results = call(
-        functools.partial(ffn_kernel, chunk, ring),
-        [block] * experts,
-        [VMEM] * (experts + 2) + [HBM],
+    head = min(HEAD, hidden_units)
+    weights, up_here = call(
+        functools.partial(weigh_kernel, head),
+        [pltpu.VMEM((TERMS * tokens, slots), bf16), pltpu.VMEM((width, hidden_units), bf16)],
+        [VMEM] * 3 + [HBM],
+        flops=10**6,
+        moved=2 * width * head,
+        scratch=[pltpu.SemaphoreType.DMA],
+    )(in_vmem(normed), router_rows, in_vmem(routes_here), in_hbm(w_up[0, 0]))
+    *results, _ = call(
+        functools.partial(ffn_kernel, experts, CHUNK, BAND, head),
+        [block] * experts + [pltpu.VMEM((width, hidden_units), bf16)],
+        [VMEM] * (experts + 2) + [HBM, HBM],
         flops=6 * slots * width * hidden_units,
         moved=6 * width * hidden_units,
         limit=6 * MIB,
         scratch=[
             pltpu.VMEM((slots, width), bf16),
-            pltpu.VMEM((slots, width), jnp.float32),
-            pltpu.VMEM((ring, piece, width), bf16),
-            pltpu.SemaphoreType.DMA((ring,)),
+            pltpu.VMEM((slots, hidden_units), bf16),
+            pltpu.SemaphoreType.DMA((2 * hidden_units // BAND,)),
+            pltpu.SemaphoreType.DMA((max(1, (hidden_units - head) // CHUNK),)),
         ],
-    )(*map(in_vmem, arrived), *weights_in)
+        aliases={experts + 1: experts},
+    )(*map(in_vmem, arrived), in_vmem(w_gate[0, 0]), in_vmem(up_here), in_hbm(w_up[0, 0]), in_hbm(w_down[0, 0]))
     returned = [swapped(result, k) if k else result for result, k in zip(results, order)]
     out = call(
         functools.partial(combine_kernel, order),
@@ -307,7 +334,9 @@
 
 def per_device(*args):
     experts = args[4].shape[2]
+    width, hidden_units = args[5].shape[2:]
     alone = lax.axis_size("expert") == experts and experts & (experts - 1) == 0
+    alone &= hidden_units % CHUNK == 0 and hidden_units % (width // 2) == 0 and width % (2 * BAND) == 0
     return (one_expert_each if alone else shared_experts)(*args)
 
 

time: 62.7 us -> 55.4 us (0.88)
  waiting for transfers between devices: 8.21 us -> 4.04 us
  local copies, waits for them, and re-layouts: 2.74 us -> 0.04 us
  Pallas kernels: 24.3 us -> 23.2 us
  starting transfers between devices: 26.5 us -> 27.2 us
    ppermute x14, waiting for transfers between devices: 6.93 us -> 2.97 us  [swapped(): return lax.ppermute(x, 'expert', [(i, i ^ k) for i in range(length)])]
    unnamed x6 -> x16, local copies, waits for them, and re-layouts: 2.74 us -> 0.04 us
    pallas_call x3, Pallas kernels: 22.3 us -> 21.2 us  [the longest x1 15 us: one_expert_each(): call(functools.partial(ffn_kernel, experts, CHUNK, BAND, head), [block] *...]
    ppermute x14, starting transfers between devices: 22 us -> 22.7 us  [swapped(): return lax.ppermute(x, 'expert', [(i, i ^ k) for i in range(length)])]
  transfers between devices with their start and end apart: 15 -> 15, of which waited for: 7 -> 4; matrix products, arithmetic and copies ran while one was open for 0% -> 0% of each run, Pallas kernels for 2% -> 13%
where the time goes in v2:
time: 55.4 us; the launch traced here: 54.7 us
  starting transfers between devices  27.2 us (49%)
  Pallas kernels  23.2 us (42%)
  waiting for transfers between devices  4.04 us (7%)
    ppermute x14, starting transfers between devices, swapped(): return lax.ppermute(x, 'expert', [(i, i ^ k) for i in range(length)])  22.7 us
    pallas_call x1, Pallas kernels, one_expert_each(): call(functools.partial(ffn_kernel, experts, CHUNK, BAND, head), [block] *...  15 us
    pallas_call x1, Pallas kernels, one_expert_each(): call(functools.partial(weigh_kernel, head), [pltpu.VMEM((TERMS * tokens,...  5.79 us
    ppermute x1, starting transfers between devices, passed_along(): return lax.ppermute(x, axis, pairs)  4.5 us
    ppermute x14, waiting for transfers between devices, swapped(): return lax.ppermute(x, 'expert', [(i, i ^ k) for i in range(length)])  2.97 us
  transfers between devices with their start and end apart: 15, of which 4 were waited for; matrix products, arithmetic and copies ran while one was open for 0% of the time, Pallas kernels for 13%

profile of v2, /device:TPU:1, one launch (start us, length us, event | category | flops | bytes accessed | tf_op | source)
XLA Modules:
  0.0 54.7 jit_solution(11877312673391219174)
XLA Ops:
  0.0 4.5 %collective-permute-start = (bf16[32,2048]{1,0:T(8,128)(2,1)}, bf16[32,2048]{1,0:T(8,128)(2,1)S(1)}, u32[]{:S(2)}, u32[]{:S(2)}) collective-permute-start(bf16[32,2048]{1,0:T(8,128)(2,1)} %bitcast.18), channel_id=1, source_target_pairs={{0,8},{8,16},{16,24},{1,9},{9,17},{17,25},{2,10},{10,18},{18,26},{... | collective-permute-start | bytes 393224 | tf_op jit(solution)/shard_map/ppermute | solution.py:21
  4.5 0.0 slice-start
  4.5 0.0 copy-start
  4.5 0.0 slice-start.1
  4.5 0.0 slice-start.2
  4.5 0.0 slice-start.3
  4.6 0.0 slice-start.4
  4.6 0.0 slice-start.5
  4.6 0.0 slice-start.6
  4.6 1.1 %shard_map.82 = (bf16[128,32]{1,0:T(8,128)(2,1)S(1)}, bf16[32,2048]{1,0:T(8,128)(2,1)S(1)}, s32[2,32]{1,0:T(2,128)S(1)}, f32[1,2048]{1,0:T(1,128)S(1)}) custom-call(bf16[32,2048]{1,0:T(8,128)(2,1)} %fresh.1, s32[2,32]{1,0:T(2,128)} %bitcast.19, f32[1,2048]{1,0:T(1,128)} %gain.1), custom_call_target="tpu_custom_call" | custom-call | flops 60000002048 | bytes 1000000 | tf_op jit(solution)/shard_map/pallas_call | solution.py:212
  5.7 1.1 %collective-permute-done.received = bf16[32,2048]{1,0:T(8,128)(2,1)S(1)} collective-permute-done((bf16[32,2048]{1,0:T(8,128)(2,1)}, bf16[32,2048]{1,0:T(8,128)(2,1)S(1)}, u32[]{:S(2)}, u32[]{:S(2)}) %collective-permute-start) | collective-permute-done | bytes 131104 | tf_op jit(solution)/shard_map/ppermute | solution.py:21
  6.7 0.4 shard_map.83
  7.2 4.3 %collective-permute-start.1 = (bf16[16,2048]{1,0:T(8,128)(2,1)S(1)}, bf16[16,2048]{1,0:T(8,128)(2,1)S(1)}, u32[]{:S(2)}, u32[]{:S(2)}) collective-permute-start(bf16[16,2048]{1,0:T(8,128)(2,1)S(1)} %get-tuple-element.36), channel_id=1, source_target_pairs={{0,7},{1,6},{2,5},{3,4},{4,3},{5,2},{6,1},{7,0},{8,15},{9,14},{10,... | collective-permute-start | bytes 196616 | tf_op jit(solution)/shard_map/ppermute | solution.py:26
  11.5 0.0 collective-permute-start.2
  11.5 0.4 collective-permute-start.3
  11.9 2.0 %collective-permute-start.4 = (bf16[16,2048]{1,0:T(8,128)(2,1)S(1)}, bf16[16,2048]{1,0:T(8,128)(2,1)S(1)}, u32[]{:S(2)}, u32[]{:S(2)}) collective-permute-start(bf16[16,2048]{1,0:T(8,128)(2,1)S(1)} %get-tuple-element.39), channel_id=1, source_target_pairs={{0,4},{1,5},{2,6},{3,7},{4,0},{5,1},{6,2},{7,3},{8,12},{9,13},{10,... | collective-permute-start | bytes 196616 | tf_op jit(solution)/shard_map/ppermute | solution.py:26
  13.9 2.0 %collective-permute-start.5 = (bf16[16,2048]{1,0:T(8,128)(2,1)S(1)}, bf16[16,2048]{1,0:T(8,128)(2,1)S(1)}, u32[]{:S(2)}, u32[]{:S(2)}) collective-permute-start(bf16[16,2048]{1,0:T(8,128)(2,1)S(1)} %get-tuple-element.40), channel_id=1, source_target_pairs={{0,3},{1,2},{2,1},{3,0},{4,7},{5,6},{6,5},{7,4},{8,11},{9,10},{10,... | collective-permute-start | bytes 196616 | tf_op jit(solution)/shard_map/ppermute | solution.py:26
  16.0 0.0 collective-permute-done.1.refs_0_
  16.0 2.2 %collective-permute-start.6 = (bf16[16,2048]{1,0:T(8,128)(2,1)S(1)}, bf16[16,2048]{1,0:T(8,128)(2,1)S(1)}, u32[]{:S(2)}, u32[]{:S(2)}) collective-permute-start(bf16[16,2048]{1,0:T(8,128)(2,1)S(1)} %get-tuple-element.41), channel_id=1, source_target_pairs={{0,2},{1,3},{2,0},{3,1},{4,6},{5,7},{6,4},{7,5},{8,10},{9,11},{10,... | collective-permute-start | bytes 196616 | tf_op jit(solution)/shard_map/ppermute | solution.py:26
  18.1 0.0 collective-permute-done.2.refs_1_
  18.1 0.0 collective-permute-start.7
  18.1 0.0 copy-done
  18.2 5.8 %shard_map.84 = (bf16[96,128]{1,0:T(8,128)(2,1)S(1)}, bf16[2048,7168]{1,0:T(8,128)(2,1)S(1)}) custom-call(bf16[32,2048]{1,0:T(8,128)(2,1)S(1)} %get-tuple-element.33.normed, bf16[8,2048]{1,0:T(8,128)(2,1)S(1)} %bitcast.14, s32[2,32]{1,0:T(2,128)S(1)} %get-tuple-element.34.routes, bf16[2048,7168]{1,0:T(8,128)(2,1)} %bitcast.15), custom_call_target="tpu_custom_call" | custom-call | flops 1000000 | bytes 16777216 | tf_op jit(solution)/shard_map/pallas_call | solution.py:233
  23.9 0.0 collective-permute-done.3.refs_2_
  24.0 0.0 collective-permute-done.4.refs_3_
  24.0 0.0 collective-permute-done.5.refs_4_
  24.0 0.0 collective-permute-done.6.refs_5_
  24.0 0.0 collective-permute-done.7.refs_6_
  24.0 0.0 slice-done
  24.0 0.0 slice-done.1
  24.0 0.0 slice-done.2
  24.0 0.0 slice-done.3
  24.0 0.0 slice-done.4
  24.1 0.0 slice-done.5
  24.1 0.0 slice-done.6
  24.1 15.0 %shard_map.85 = (bf16[16,2048]{1,0:T(8,128)(2,1)S(1)}, bf16[16,2048]{1,0:T(8,128)(2,1)S(1)}, bf16[16,2048]{1,0:T(8,128)(2,1)S(1)}, bf16[16,2048]{1,0:T(8,128)(2,...) custom-call(bf16[16,2048]{1,0:T(8,128)(2,1)S(1)} %collective-permute, ...), custom_call_target="tpu_custom_call", output_to_operand_aliasing={{8}: (9, {})} | custom-call | flops 11274289152 | bytes 88080384 | tf_op jit(solution)/shard_map/pallas_call | solution.py:241
  39.1 4.0 %collective-permute-start.8 = (bf16[16,2048]{1,0:T(8,128)(2,1)S(1)}, bf16[16,2048]{1,0:T(8,128)(2,1)S(1)}, u32[]{:S(2)}, u32[]{:S(2)}) collective-permute-start(bf16[16,2048]{1,0:T(8,128)(2,1)S(1)} %get-tuple-element.45), channel_id=1, source_target_pairs={{0,7},{1,6},{2,5},{3,4},{4,3},{5,2},{6,1},{7,0},{8,15},{9,14},{10,... | collective-permute-start | bytes 196616 | tf_op jit(solution)/shard_map/ppermute | solution.py:26
  43.1 0.5 collective-permute-start.9
  43.6 1.2 %collective-permute-start.10 = (bf16[16,2048]{1,0:T(8,128)(2,1)S(1)}, bf16[16,2048]{1,0:T(8,128)(2,1)S(1)}, u32[]{:S(2)}, u32[]{:S(2)}) collective-permute-start(bf16[16,2048]{1,0:T(8,128)(2,1)S(1)} %get-tuple-element.47), channel_id=1, source_target_pairs={{0,5},{1,4},{2,7},{3,6},{4,1},{5,0},{6,3},{7,2},{8,13},{9,12},{10,... | collective-permute-start | bytes 196616 | tf_op jit(solution)/shard_map/ppermute | solution.py:26
  44.8 1.8 %collective-permute-start.11 = (bf16[16,2048]{1,0:T(8,128)(2,1)S(1)}, bf16[16,2048]{1,0:T(8,128)(2,1)S(1)}, u32[]{:S(2)}, u32[]{:S(2)}) collective-permute-start(bf16[16,2048]{1,0:T(8,128)(2,1)S(1)} %get-tuple-element.48), channel_id=1, source_target_pairs={{0,4},{1,5},{2,6},{3,7},{4,0},{5,1},{6,2},{7,3},{8,12},{9,13},{10,... | collective-permute-start | bytes 196616 | tf_op jit(solution)/shard_map/ppermute | solution.py:26
  46.6 1.2 %collective-permute-start.12 = (bf16[16,2048]{1,0:T(8,128)(2,1)S(1)}, bf16[16,2048]{1,0:T(8,128)(2,1)S(1)}, u32[]{:S(2)}, u32[]{:S(2)}) collective-permute-start(bf16[16,2048]{1,0:T(8,128)(2,1)S(1)} %get-tuple-element.49), channel_id=1, source_target_pairs={{0,3},{1,2},{2,1},{3,0},{4,7},{5,6},{6,5},{7,4},{8,11},{9,10},{10,... | collective-permute-start | bytes 196616 | tf_op jit(solution)/shard_map/ppermute | solution.py:26
  47.8 0.0 collective-permute-done.8.refs_0_
  47.8 2.6 %collective-permute-start.13 = (bf16[16,2048]{1,0:T(8,128)(2,1)S(1)}, bf16[16,2048]{1,0:T(8,128)(2,1)S(1)}, u32[]{:S(2)}, u32[]{:S(2)}) collective-permute-start(bf16[16,2048]{1,0:T(8,128)(2,1)S(1)} %get-tuple-element.50), channel_id=1, source_target_pairs={{0,2},{1,3},{2,0},{3,1},{4,6},{5,7},{6,4},{7,5},{8,10},{9,11},{10,... | collective-permute-start | bytes 196616 | tf_op jit(solution)/shard_map/ppermute | solution.py:26
  50.4 0.0 collective-permute-done.9.refs_1_
  50.4 0.4 collective-permute-start.14
  50.8 1.6 %collective-permute-done.10.refs_2_ = bf16[16,2048]{1,0:T(8,128)(2,1)S(1)} collective-permute-done((bf16[16,2048]{1,0:T(8,128)(2,1)S(1)}, bf16[16,2048]{1,0:T(8,128)(2,1)S(1)}, u32[]{:S(2)}, u32[]{:S(2)}) %collective-permute-start.10) | collective-permute-done | bytes 65568 | tf_op jit(solution)/shard_map/ppermute | solution.py:26
  52.4 1.1 %collective-permute-done.11.refs_3_ = bf16[16,2048]{1,0:T(8,128)(2,1)S(1)} collective-permute-done((bf16[16,2048]{1,0:T(8,128)(2,1)S(1)}, bf16[16,2048]{1,0:T(8,128)(2,1)S(1)}, u32[]{:S(2)}, u32[]{:S(2)}) %collective-permute-start.11) | collective-permute-done | bytes 65568 | tf_op jit(solution)/shard_map/ppermute | solution.py:26
  53.5 0.0 collective-permute-done.12.refs_4_
  53.5 0.3 collective-permute-done.13.refs_5_
  53.8 0.0 collective-permute-done.14.refs_6_
  53.8 0.9 %shard_map.86 = bf16[32,2048]{1,0:T(8,128)(2,1)} custom-call(bf16[32,2048]{1,0:T(8,128)(2,1)S(1)} %get-tuple-element.32.inputs, bf16[96,128]{1,0:T(8,128)(2,1)S(1)} %get-tuple-element.35.weights, bf16[16,2048]{1,0:T(8,128)(2,1)S(1)} %collective-permute-done.8.refs_0_, bf16[16,2048]{1,0:T(8,128)(2,1)S(1)} %collective-permute-done.9.refs_1_, ...), custom_call_target="tpu_custom_call" | custom-call | flops 100000000 | bytes 1000000 | tf_op jit(solution)/shard_map/pallas_call | solution.py:257
  (1 shorter events, 0.0 us)
Async XLA Ops:
  0.0 6.7 %collective-permute-start = (bf16[32,2048]{1,0:T(8,128)(2,1)}, bf16[32,2048]{1,0:T(8,128)(2,1)S(1)}, u32[]{:S(2)}, u32[]{:S(2)}) collective-permute-start(bf16[32,2048]{1,0:T(8,128)(2,1)} %bitcast.18), channel_id=1, source_target_pairs={{0,8},{8,16},{16,24},{1,9},{9,17},{17,25},{2,10},{10,18},{18,26},{... | collective-permute-start | bytes 393224 | tf_op jit(solution)/shard_map/ppermute | solution.py:21
  4.5 19.5 %slice-start = ((s8[29360128]{0:T(1024)(128)(4,1)}), s8[4194304]{0:T(1024)(128)(4,1)S(1)}, s32[]{:S(2)}) async-start(s8[29360128]{0:T(1024)(128)(4,1)} %bitcast.11), calls=%async_computation | async-start | bytes 8388608
  4.5 13.6 %copy-start = (bf16[1,2048,8]{1,2,0:T(8,128)(2,1)S(1)}, bf16[1,2048,8]{1,2,0:T(8,128)(2,1)}, u32[]{:S(2)}) copy-start(bf16[1,2048,8]{1,2,0:T(8,128)(2,1)} %param.12) | copy-start | bytes 98308
  4.5 19.5 %slice-start.1 = ((s8[29360128]{0:T(1024)(128)(4,1)}), s8[4194304]{0:T(1024)(128)(4,1)S(1)}, s32[]{:S(2)}) async-start(s8[29360128]{0:T(1024)(128)(4,1)} %bitcast.11), calls=%async_computation.1 | async-start | bytes 8388608
  4.5 19.5 %slice-start.2 = ((s8[29360128]{0:T(1024)(128)(4,1)}), s8[4194304]{0:T(1024)(128)(4,1)S(1)}, s32[]{:S(2)}) async-start(s8[29360128]{0:T(1024)(128)(4,1)} %bitcast.11), calls=%async_computation.2 | async-start | bytes 8388608
  4.5 19.5 %slice-start.3 = ((s8[29360128]{0:T(1024)(128)(4,1)}), s8[4194304]{0:T(1024)(128)(4,1)S(1)}, s32[]{:S(2)}) async-start(s8[29360128]{0:T(1024)(128)(4,1)} %bitcast.11), calls=%async_computation.3 | async-start | bytes 8388608
  4.6 19.5 %slice-start.4 = ((s8[29360128]{0:T(1024)(128)(4,1)}), s8[4194304]{0:T(1024)(128)(4,1)S(1)}, s32[]{:S(2)}) async-start(s8[29360128]{0:T(1024)(128)(4,1)} %bitcast.11), calls=%async_computation.4 | async-start | bytes 8388608
  4.6 19.5 %slice-start.5 = ((s8[29360128]{0:T(1024)(128)(4,1)}), s8[4194304]{0:T(1024)(128)(4,1)S(1)}, s32[]{:S(2)}) async-start(s8[29360128]{0:T(1024)(128)(4,1)} %bitcast.11), calls=%async_computation.5 | async-start | bytes 8388608
  4.6 19.5 %slice-start.6 = ((s8[29360128]{0:T(1024)(128)(4,1)}), s8[4194304]{0:T(1024)(128)(4,1)S(1)}, s32[]{:S(2)}) async-start(s8[29360128]{0:T(1024)(128)(4,1)} %bitcast.11), calls=%async_computation.6 | async-start | bytes 8388608
  7.2 8.8 %collective-permute-start.1 = (bf16[16,2048]{1,0:T(8,128)(2,1)S(1)}, bf16[16,2048]{1,0:T(8,128)(2,1)S(1)}, u32[]{:S(2)}, u32[]{:S(2)}) collective-permute-start(bf16[16,2048]{1,0:T(8,128)(2,1)S(1)} %get-tuple-element.36), channel_id=1, source_target_pairs={{0,7},{1,6},{2,5},{3,4},{4,3},{5,2},{6,1},{7,0},{8,15},{9,14},{10,... | collective-permute-start | bytes 196616 | tf_op jit(solution)/shard_map/ppermute | solution.py:26
  11.5 6.6 %collective-permute-start.2 = (bf16[16,2048]{1,0:T(8,128)(2,1)S(1)}, bf16[16,2048]{1,0:T(8,128)(2,1)S(1)}, u32[]{:S(2)}, u32[]{:S(2)}) collective-permute-start(bf16[16,2048]{1,0:T(8,128)(2,1)S(1)} %get-tuple-element.37), channel_id=1, source_target_pairs={{0,6},{1,7},{2,4},{3,5},{4,2},{5,3},{6,0},{7,1},{8,14},{9,15},{10,... | collective-permute-start | bytes 196616 | tf_op jit(solution)/shard_map/ppermute | solution.py:26
  11.5 12.4 %collective-permute-start.3 = (bf16[16,2048]{1,0:T(8,128)(2,1)S(1)}, bf16[16,2048]{1,0:T(8,128)(2,1)S(1)}, u32[]{:S(2)}, u32[]{:S(2)}) collective-permute-start(bf16[16,2048]{1,0:T(8,128)(2,1)S(1)} %get-tuple-element.38), channel_id=1, source_target_pairs={{0,5},{1,4},{2,7},{3,6},{4,1},{5,0},{6,3},{7,2},{8,13},{9,12},{10,... | collective-permute-start | bytes 196616 | tf_op jit(solution)/shard_map/ppermute | solution.py:26
  11.9 12.1 %collective-permute-start.4 = (bf16[16,2048]{1,0:T(8,128)(2,1)S(1)}, bf16[16,2048]{1,0:T(8,128)(2,1)S(1)}, u32[]{:S(2)}, u32[]{:S(2)}) collective-permute-start(bf16[16,2048]{1,0:T(8,128)(2,1)S(1)} %get-tuple-element.39), channel_id=1, source_target_pairs={{0,4},{1,5},{2,6},{3,7},{4,0},{5,1},{6,2},{7,3},{8,12},{9,13},{10,... | collective-permute-start | bytes 196616 | tf_op jit(solution)/shard_map/ppermute | solution.py:26
  13.9 10.0 %collective-permute-start.5 = (bf16[16,2048]{1,0:T(8,128)(2,1)S(1)}, bf16[16,2048]{1,0:T(8,128)(2,1)S(1)}, u32[]{:S(2)}, u32[]{:S(2)}) collective-permute-start(bf16[16,2048]{1,0:T(8,128)(2,1)S(1)} %get-tuple-element.40), channel_id=1, source_target_pairs={{0,3},{1,2},{2,1},{3,0},{4,7},{5,6},{6,5},{7,4},{8,11},{9,10},{10,... | collective-permute-start | bytes 196616 | tf_op jit(solution)/shard_map/ppermute | solution.py:26
  16.0 8.0 %collective-permute-start.6 = (bf16[16,2048]{1,0:T(8,128)(2,1)S(1)}, bf16[16,2048]{1,0:T(8,128)(2,1)S(1)}, u32[]{:S(2)}, u32[]{:S(2)}) collective-permute-start(bf16[16,2048]{1,0:T(8,128)(2,1)S(1)} %get-tuple-element.41), channel_id=1, source_target_pairs={{0,2},{1,3},{2,0},{3,1},{4,6},{5,7},{6,4},{7,5},{8,10},{9,11},{10,... | collective-permute-start | bytes 196616 | tf_op jit(solution)/shard_map/ppermute | solution.py:26
  18.1 5.8 %collective-permute-start.7 = (bf16[16,2048]{1,0:T(8,128)(2,1)S(1)}, bf16[16,2048]{1,0:T(8,128)(2,1)S(1)}, u32[]{:S(2)}, u32[]{:S(2)}) collective-permute-start(bf16[16,2048]{1,0:T(8,128)(2,1)S(1)} %get-tuple-element.42), channel_id=1, source_target_pairs={{0,1},{1,0},{2,3},{3,2},{4,5},{5,4},{6,7},{7,6},{8,9},{9,8},{10,11... | collective-permute-start | bytes 196616 | tf_op jit(solution)/shard_map/ppermute | solution.py:26
  39.1 8.7 %collective-permute-start.8 = (bf16[16,2048]{1,0:T(8,128)(2,1)S(1)}, bf16[16,2048]{1,0:T(8,128)(2,1)S(1)}, u32[]{:S(2)}, u32[]{:S(2)}) collective-permute-start(bf16[16,2048]{1,0:T(8,128)(2,1)S(1)} %get-tuple-element.45), channel_id=1, source_target_pairs={{0,7},{1,6},{2,5},{3,4},{4,3},{5,2},{6,1},{7,0},{8,15},{9,14},{10,... | collective-permute-start | bytes 196616 | tf_op jit(solution)/shard_map/ppermute | solution.py:26
  43.1 7.4 %collective-permute-start.9 = (bf16[16,2048]{1,0:T(8,128)(2,1)S(1)}, bf16[16,2048]{1,0:T(8,128)(2,1)S(1)}, u32[]{:S(2)}, u32[]{:S(2)}) collective-permute-start(bf16[16,2048]{1,0:T(8,128)(2,1)S(1)} %get-tuple-element.46), channel_id=1, source_target_pairs={{0,6},{1,7},{2,4},{3,5},{4,2},{5,3},{6,0},{7,1},{8,14},{9,15},{10,... | collective-permute-start | bytes 196616 | tf_op jit(solution)/shard_map/ppermute | solution.py:26
  43.6 8.8 %collective-permute-start.10 = (bf16[16,2048]{1,0:T(8,128)(2,1)S(1)}, bf16[16,2048]{1,0:T(8,128)(2,1)S(1)}, u32[]{:S(2)}, u32[]{:S(2)}) collective-permute-start(bf16[16,2048]{1,0:T(8,128)(2,1)S(1)} %get-tuple-element.47), channel_id=1, source_target_pairs={{0,5},{1,4},{2,7},{3,6},{4,1},{5,0},{6,3},{7,2},{8,13},{9,12},{10,... | collective-permute-start | bytes 196616 | tf_op jit(solution)/shard_map/ppermute | solution.py:26
  44.8 8.7 %collective-permute-start.11 = (bf16[16,2048]{1,0:T(8,128)(2,1)S(1)}, bf16[16,2048]{1,0:T(8,128)(2,1)S(1)}, u32[]{:S(2)}, u32[]{:S(2)}) collective-permute-start(bf16[16,2048]{1,0:T(8,128)(2,1)S(1)} %get-tuple-element.48), channel_id=1, source_target_pairs={{0,4},{1,5},{2,6},{3,7},{4,0},{5,1},{6,2},{7,3},{8,12},{9,13},{10,... | collective-permute-start | bytes 196616 | tf_op jit(solution)/shard_map/ppermute | solution.py:26
  46.6 6.9 %collective-permute-start.12 = (bf16[16,2048]{1,0:T(8,128)(2,1)S(1)}, bf16[16,2048]{1,0:T(8,128)(2,1)S(1)}, u32[]{:S(2)}, u32[]{:S(2)}) collective-permute-start(bf16[16,2048]{1,0:T(8,128)(2,1)S(1)} %get-tuple-element.49), channel_id=1, source_target_pairs={{0,3},{1,2},{2,1},{3,0},{4,7},{5,6},{6,5},{7,4},{8,11},{9,10},{10,... | collective-permute-start | bytes 196616 | tf_op jit(solution)/shard_map/ppermute | solution.py:26
  47.8 6.0 %collective-permute-start.13 = (bf16[16,2048]{1,0:T(8,128)(2,1)S(1)}, bf16[16,2048]{1,0:T(8,128)(2,1)S(1)}, u32[]{:S(2)}, u32[]{:S(2)}) collective-permute-start(bf16[16,2048]{1,0:T(8,128)(2,1)S(1)} %get-tuple-element.50), channel_id=1, source_target_pairs={{0,2},{1,3},{2,0},{3,1},{4,6},{5,7},{6,4},{7,5},{8,10},{9,11},{10,... | collective-permute-start | bytes 196616 | tf_op jit(solution)/shard_map/ppermute | solution.py:26
  50.4 3.3 %collective-permute-start.14 = (bf16[16,2048]{1,0:T(8,128)(2,1)S(1)}, bf16[16,2048]{1,0:T(8,128)(2,1)S(1)}, u32[]{:S(2)}, u32[]{:S(2)}) collective-permute-start(bf16[16,2048]{1,0:T(8,128)(2,1)S(1)} %get-tuple-element.51), channel_id=1, source_target_pairs={{0,1},{1,0},{2,3},{3,2},{4,5},{5,4},{6,7},{7,6},{8,9},{9,8},{10,11... | collective-permute-start | bytes 196616 | tf_op jit(solution)/shard_map/ppermute | solution.py:26

commit v3 on v2

--- a/solution.py
+++ b/solution.py
@@ -48,13 +48,25 @@
     return (values * lax.rsqrt(mean_square + 1e-05) * gain).astype(jnp.bfloat16)
 
 
+def tile_comes_late():
+    section = lax.axis_index("pipe")
+    return (section > 0) & (section < lax.axis_size("pipe") - 1)
+
+
 def prepare_kernel(
-    experts, capacity, fresh, routes, gain, placing, fresh_here, routes_here, gain_here, sems
+    experts, capacity, fresh, routes, gain, up, placing, fresh_here, routes_here, gain_here, first, sems
 ):
     pairs = ((routes, routes_here), (fresh, fresh_here), (gain, gain_here))
     copies = [pltpu.make_async_copy(a, b, sems.at[i]) for i, (a, b) in enumerate(pairs)]
     for copy in copies:
         copy.start()
+
+    @pl.when(tile_comes_late())
+    def _():
+        fetch = pltpu.make_async_copy(up.at[:, : first.shape[1]], first, sems.at[len(pairs)])
+        fetch.start()
+        fetch.wait()
+
     copies[0].wait()
     placing[...] = slot_hits(routes_here[...], experts, capacity, None).astype(jnp.bfloat16)
     for copy in copies[1:]:
@@ -73,9 +85,14 @@
         block[...] = packed[k * capacity : (k + 1) * capacity]
 
 
-def weigh_kernel(head, normed, router, routes, up, weights, up_here, sem):
-    fetch = pltpu.make_async_copy(up.at[:, :head], up_here.at[:, :head], sem)
+def weigh_kernel(first, head, normed, router, routes, up, weights, rest, sems):
+    chunk = first
+    fetch = pltpu.make_async_copy(up.at[:, chunk:head], rest.at[:, : head - chunk], sems.at[0])
     fetch.start()
+    more = pltpu.make_async_copy(
+        up.at[:, head : head + chunk], rest.at[:, head - chunk : head], sems.at[1]
+    )
+    pl.when(~tile_comes_late())(more.start)
     experts = router.shape[0]
     slots = weights.shape[1]
     logits = lax.dot_general(
@@ -104,57 +121,87 @@
         ).astype(jnp.bfloat16)
         total = total - part.astype(jnp.float32)
     fetch.wait()
-
-
-def ffn_kernel(count, chunk, band, head, *refs):
-    blocks, (gate, _, up, down) = refs[:count], refs[count : count + 4]
-    outs = refs[count + 4 : 2 * count + 4]
-    spare, rows, hidden, sems, tail_sems = refs[2 * count + 4 :]
+    pl.when(~tile_comes_late())(more.wait)
+
+
+def first_chunk(c):
+    return isinstance(c, int) and c == 0
+
+
+def ffn_kernel(count, band, head, *refs):
+    blocks, (gate, _, _, up, down) = refs[:count], refs[count : count + 5]
+    outs, spares = refs[count + 5 : 2 * count + 5], refs[2 * count + 5 : 2 * count + 7]
+    rows, hidden, sems, tail_sems = refs[2 * count + 7 :]
     capacity = blocks[0].shape[0]
     width, hidden_units = gate.shape
+    chunk = spares[0].shape[1]
     unit = width // 2
     tall = hidden_units // unit
-
-    def place(u):
-        return pl.ds(u % 2 * unit, unit), pl.ds(u // 2 * band, band)
-
-    def fetch(u):
-        source = down.at[pl.ds(u % tall * unit, unit), pl.ds(u // tall * band, band)]
-        return pltpu.make_async_copy(source, spare.at[place(u)], sems.at[u])
-
-    def fetch_tail(c):
-        columns = pl.ds(pl.multiple_of(c * chunk, chunk), chunk)
-        return pltpu.make_async_copy(up.at[:, columns], spare.at[:, columns], tail_sems.at[c - head // chunk])
-
-    for c in range(head // chunk, hidden_units // chunk):
-        fetch_tail(c).start()
+    per_chunk = 2 * chunk // band
+    loaded, chunks = head // chunk, hidden_units // chunk
+    order = [*range(1, loaded), *range(loaded + 1, chunks), 0, loaded]
+
+    def place(u, c):
+        late = int(not first_chunk(c))
+        left = (c - 1) * chunk if late else 0
+        columns = pl.ds(pl.multiple_of(left + u % per_chunk // 2 * band, band), band)
+        return spares[late].at[pl.ds(u % 2 * unit, unit), columns]
+
+    def fetch(u, c):
+        source = down.at[pl.ds(u % tall * unit, unit), pl.ds(pl.multiple_of(u // tall * band, band), band)]
+        return pltpu.make_async_copy(source, place(u, c), sems.at[u])
+
+    def columns_of(c):
+        return pl.ds(pl.multiple_of(c * chunk, chunk), chunk)
+
+    def part_of(c):
+        return spares[0] if first_chunk(c) else spares[1].at[:, columns_of(c - 1)]
+
+    def fetch_tail(c, slot):
+        return pltpu.make_async_copy(up.at[:, columns_of(c)], part_of(c), tail_sems.at[slot])
+
+    for c in range(loaded + 1, chunks):
+        fetch_tail(c, c - loaded).start()
+    pl.when(tile_comes_late())(fetch_tail(loaded, 0).start)
+    pl.when(~tile_comes_late())(fetch_tail(0, 0).start)
     for k in range(count):
         rows[k * capacity : (k + 1) * capacity, :] = blocks[k][...]
 
-    def step(c, fetched):
-        columns = pl.ds(pl.multiple_of(c * chunk, chunk), chunk)
+    def step(c, turn):
         x = rows[...]
-        if not fetched:
-            fetch_tail(c).wait()
-        gate_proj = jnp.dot(x, gate[:, columns], preferred_element_type=jnp.float32)
-
-        up_proj = jnp.dot(x, spare[:, columns], preferred_element_type=jnp.float32)
-        hidden[:, columns] = (jax.nn.silu(gate_proj) * up_proj).astype(jnp.bfloat16)
-        for j in range(2 * chunk // band):
-            fetch(c * (2 * chunk // band) + j).start()
-
-    pl.loop(0, head // chunk)(lambda c: step(c, True))
-    pl.loop(head // chunk, hidden_units // chunk)(lambda c: step(c, False))
+        gate_proj = jnp.dot(x, gate[:, columns_of(c)], preferred_element_type=jnp.float32)
+        up_proj = jnp.dot(x, part_of(c)[...], preferred_element_type=jnp.float32)
+        hidden[:, columns_of(c)] = (jax.nn.silu(gate_proj) * up_proj).astype(jnp.bfloat16)
+        for j in range(per_chunk):
+            fetch(turn * per_chunk + j, c).start()
+
+    @pl.loop(0, loaded - 1)
+    def _(turn):
+        step(turn + 1, turn)
+
+    @pl.loop(loaded - 1, chunks - 2)
+    def _(turn):
+        fetch_tail(turn + 2, turn + 2 - loaded).wait()
+        step(turn + 2, turn)
+
+    fetch_tail(0, 0).wait()
+    step(0, chunks - 2)
+    step(loaded, chunks - 1)
     for j in range(width // band):
         total, u = None, j * tall
+        last = j == width // band - 1
+        if not last:
+            for v in range(u, u + tall):
+                fetch(v, order[v // per_chunk]).wait()
         while u < (j + 1) * tall:
             paired = u % 2 == 0 and u + 1 < (j + 1) * tall
-            for v in range(u, u + 1 + paired):
-                fetch(v).wait()
-            start, columns = u % 2 * unit, place(u)[1]
+            c = order[u // per_chunk]
+            for v in range(u, u + 1 + paired) if last else ():
+                fetch(v, c).wait()
+            top, left = u % 2 * unit, u % per_chunk // 2 * band
             part = jnp.dot(
                 hidden[:, u % tall * unit : (u % tall + 1 + paired) * unit],
-                spare[start : start + (1 + paired) * unit, columns],
+                part_of(c)[top : top + (1 + paired) * unit, left : left + band],
                 preferred_element_type=jnp.float32,
             )
             total = part if total is None else total + part
@@ -209,19 +256,20 @@
     chosen = jnp.transpose(routes[0])
     router_rows = jnp.transpose(router[0])
     received = passed_along(held[0], "pipe", 1)
-    placing, fresh_here, routes_here, gain_here = call(
+    placing, fresh_here, routes_here, gain_here, up_first = call(
         functools.partial(prepare_kernel, experts, capacity),
         [
             pltpu.VMEM((slots, tokens), bf16),
             pltpu.VMEM(fresh.shape, bf16),
             pltpu.VMEM(chosen.shape, jnp.int32),
             pltpu.VMEM(norm_gain.shape, jnp.float32),
+            pltpu.VMEM((width, CHUNK), bf16),
         ],
-        [HBM] * 3,
+        [HBM] * 4,
         flops=60 * 10**9,
         moved=10**6,
-        scratch=[pltpu.SemaphoreType.DMA((3,))],
-    )(*map(in_hbm, (fresh, chosen, norm_gain)))
+        scratch=[pltpu.SemaphoreType.DMA((4,))],
+    )(*map(in_hbm, (fresh, chosen, norm_gain, w_up[0, 0])))
     tile = pltpu.VMEM((tokens, width), bf16)
     block = pltpu.VMEM((capacity, width), bf16)
     inputs, normed, *packed = call(
@@ -229,19 +277,18 @@
     )(*map(in_vmem, (received, fresh_here, gain_here, placing)))
     order = range(experts - 1, -1, -1)
     arrived = [swapped(packed[k], k) if k else packed[k] for k in order]
-    head = min(HEAD, hidden_units)
-    weights, up_here = call(
-        functools.partial(weigh_kernel, head),
-        [pltpu.VMEM((TERMS * tokens, slots), bf16), pltpu.VMEM((width, hidden_units), bf16)],
+    weights, up_rest = call(
+        functools.partial(weigh_kernel, CHUNK, HEAD),
+        [pltpu.VMEM((TERMS * tokens, slots), bf16), pltpu.VMEM((width, hidden_units - CHUNK), bf16)],
         [VMEM] * 3 + [HBM],
         flops=10**6,
-        moved=2 * width * head,
-        scratch=[pltpu.SemaphoreType.DMA],
+        moved=2 * width * HEAD,
+        scratch=[pltpu.SemaphoreType.DMA((2,))],
     )(in_vmem(normed), router_rows, in_vmem(routes_here), in_hbm(w_up[0, 0]))
-    *results, _ = call(
-        functools.partial(ffn_kernel, experts, CHUNK, BAND, head),
-        [block] * experts + [pltpu.VMEM((width, hidden_units), bf16)],
-        [VMEM] * (experts + 2) + [HBM, HBM],
+    *results, _, _ = call(
+        functools.partial(ffn_kernel, experts, BAND, HEAD),
+        [block] * experts + [pltpu.VMEM(up.shape, bf16) for up in (up_first, up_rest)],
+        [VMEM] * (experts + 3) + [HBM, HBM],
         flops=6 * slots * width * hidden_units,
         moved=6 * width * hidden_units,
         limit=6 * MIB,
@@ -249,10 +296,10 @@
             pltpu.VMEM((slots, width), bf16),
             pltpu.VMEM((slots, hidden_units), bf16),
             pltpu.SemaphoreType.DMA((2 * hidden_units // BAND,)),
-            pltpu.SemaphoreType.DMA((max(1, (hidden_units - head) // CHUNK),)),
+            pltpu.SemaphoreType.DMA(((hidden_units - HEAD) // CHUNK,)),
         ],
-        aliases={experts + 1: experts},
-    )(*map(in_vmem, arrived), in_vmem(w_gate[0, 0]), in_vmem(up_here), in_hbm(w_up[0, 0]), in_hbm(w_down[0, 0]))
+        aliases={experts + 1: experts, experts + 2: experts + 1},
+    )(*map(in_vmem, arrived), *map(in_vmem, (w_gate[0, 0], up_first, up_rest)), *map(in_hbm, (w_up[0, 0], w_down[0, 0])))
     returned = [swapped(result, k) if k else result for result, k in zip(results, order)]
     out = call(
         functools.partial(combine_kernel, order),
@@ -336,7 +383,8 @@
     experts = args[4].shape[2]
     width, hidden_units = args[5].shape[2:]
     alone = lax.axis_size("expert") == experts and experts & (experts - 1) == 0
-    alone &= hidden_units % CHUNK == 0 and hidden_units % (width // 2) == 0 and width % (2 * BAND) == 0
+    alone &= hidden_units % CHUNK == 0 and hidden_units > HEAD + CHUNK and CHUNK % BAND == 0
+    alone &= hidden_units % (width // 2) == 0 and width % BAND == 0
     return (one_expert_each if alone else shared_experts)(*args)
 
 

time: 55.4 us -> 54.1 us (0.977)
    pallas_call x2, Pallas kernels: 20.8 us -> 18.8 us  [the longest x1 14.2 us: one_expert_each(): call(functools.partial(ffn_kernel, experts, BAND, HEAD), [block] * expert...]
    pallas_call x1, Pallas kernels: 1.09 us -> 2.59 us  [one_expert_each(): call(functools.partial(prepare_kernel, experts, capacity), [pltpu.VMEM((s...]
    ppermute x1, waiting for transfers between devices: 1.06 us -> 0.01 us  [passed_along(): return lax.ppermute(x, axis, pairs)]
    ppermute x14, waiting for transfers between devices: 2.97 us -> 3.97 us  [swapped(): return lax.ppermute(x, 'expert', [(i, i ^ k) for i in range(length)])]
  transfers between devices with their start and end apart: 15 -> 15, of which waited for: 4 -> 3; matrix products, arithmetic and copies ran while one was open for 0% -> 0% of each run, Pallas kernels for 13% -> 13%
where the time goes in v3:
time: 54.1 us; the launch traced here: 53.9 us
  starting transfers between devices  27 us (50%)
  Pallas kernels  22.7 us (42%)
  waiting for transfers between devices  3.97 us (7%)
    ppermute x14, starting transfers between devices, swapped(): return lax.ppermute(x, 'expert', [(i, i ^ k) for i in range(length)])  22.5 us
    pallas_call x1, Pallas kernels, one_expert_each(): call(functools.partial(ffn_kernel, experts, BAND, HEAD), [block] * expert...  14.2 us
    pallas_call x1, Pallas kernels, one_expert_each(): call(functools.partial(weigh_kernel, CHUNK, HEAD), [pltpu.VMEM((TERMS * t...  4.61 us
    ppermute x1, starting transfers between devices, passed_along(): return lax.ppermute(x, axis, pairs)  4.5 us
    ppermute x14, waiting for transfers between devices, swapped(): return lax.ppermute(x, 'expert', [(i, i ^ k) for i in range(length)])  3.97 us
    pallas_call x1, Pallas kernels, one_expert_each(): call(functools.partial(prepare_kernel, experts, capacity), [pltpu.VMEM((s...  2.59 us
  transfers between devices with their start and end apart: 15, of which 3 were waited for; matrix products, arithmetic and copies ran while one was open for 0% of the time, Pallas kernels for 13%

profile of v3, /device:TPU:1, one launch (start us, length us, event | category | flops | bytes accessed | tf_op | source)
XLA Modules:
  0.0 53.9 jit_solution(10734385652545836690)
XLA Ops:
  0.0 4.5 %collective-permute-start = (bf16[32,2048]{1,0:T(8,128)(2,1)}, bf16[32,2048]{1,0:T(8,128)(2,1)S(1)}, u32[]{:S(2)}, u32[]{:S(2)}) collective-permute-start(bf16[32,2048]{1,0:T(8,128)(2,1)} %bitcast.19), channel_id=1, source_target_pairs={{0,8},{8,16},{16,24},{1,9},{9,17},{17,25},{2,10},{10,18},{18,26},{... | collective-permute-start | bytes 393224 | tf_op jit(solution)/shard_map/ppermute | solution.py:21
  4.5 0.0 slice-start
  4.5 0.0 copy-start
  4.5 0.0 slice-start.1
  4.5 0.0 slice-start.2
  4.5 0.0 slice-start.3
  4.6 0.0 slice-start.4
  4.6 0.0 slice-start.5
  4.6 0.0 slice-start.6
  4.6 2.6 %shard_map.82 = (bf16[128,32]{1,0:T(8,128)(2,1)S(1)}, bf16[32,2048]{1,0:T(8,128)(2,1)S(1)}, s32[2,32]{1,0:T(2,128)S(1)}, f32[1,2048]{1,0:T(1,128)S(1)}, bf16[2048,1024]{1,0:T(8,128)(2,1)S(1)}) custom-call(bf16[32,2048]{1,0:T(8,128)(2,1)} %fresh.1, s32[2,32]{1,0:T(2,128)} %bitcast.20, f32[1,2048]{1,0:T(1,128)} %gain.1, bf16[2048,7168]{1,0:T(8,128)(2,1)} %bitcast.15), custom_call_target="tpu_custom_call" | custom-call | flops 60000002048 | bytes 1000000 | tf_op jit(solution)/shard_map/pallas_call | solution.py:259
  7.2 0.0 collective-permute-done.received
  7.2 0.4 shard_map.83
  7.6 4.3 %collective-permute-start.1 = (bf16[16,2048]{1,0:T(8,128)(2,1)S(1)}, bf16[16,2048]{1,0:T(8,128)(2,1)S(1)}, u32[]{:S(2)}, u32[]{:S(2)}) collective-permute-start(bf16[16,2048]{1,0:T(8,128)(2,1)S(1)} %get-tuple-element.37), channel_id=1, source_target_pairs={{0,7},{1,6},{2,5},{3,4},{4,3},{5,2},{6,1},{7,0},{8,15},{9,14},{10,... | collective-permute-start | bytes 196616 | tf_op jit(solution)/shard_map/ppermute | solution.py:26
  12.0 0.0 collective-permute-start.2
  12.0 0.4 collective-permute-start.3
  12.4 2.0 %collective-permute-start.4 = (bf16[16,2048]{1,0:T(8,128)(2,1)S(1)}, bf16[16,2048]{1,0:T(8,128)(2,1)S(1)}, u32[]{:S(2)}, u32[]{:S(2)}) collective-permute-start(bf16[16,2048]{1,0:T(8,128)(2,1)S(1)} %get-tuple-element.40), channel_id=1, source_target_pairs={{0,4},{1,5},{2,6},{3,7},{4,0},{5,1},{6,2},{7,3},{8,12},{9,13},{10,... | collective-permute-start | bytes 196616 | tf_op jit(solution)/shard_map/ppermute | solution.py:26
  14.4 2.0 %collective-permute-start.5 = (bf16[16,2048]{1,0:T(8,128)(2,1)S(1)}, bf16[16,2048]{1,0:T(8,128)(2,1)S(1)}, u32[]{:S(2)}, u32[]{:S(2)}) collective-permute-start(bf16[16,2048]{1,0:T(8,128)(2,1)S(1)} %get-tuple-element.41), channel_id=1, source_target_pairs={{0,3},{1,2},{2,1},{3,0},{4,7},{5,6},{6,5},{7,4},{8,11},{9,10},{10,... | collective-permute-start | bytes 196616 | tf_op jit(solution)/shard_map/ppermute | solution.py:26
  16.4 0.0 collective-permute-done.1.refs_0_
  16.4 1.6 %collective-permute-start.6 = (bf16[16,2048]{1,0:T(8,128)(2,1)S(1)}, bf16[16,2048]{1,0:T(8,128)(2,1)S(1)}, u32[]{:S(2)}, u32[]{:S(2)}) collective-permute-start(bf16[16,2048]{1,0:T(8,128)(2,1)S(1)} %get-tuple-element.42), channel_id=1, source_target_pairs={{0,2},{1,3},{2,0},{3,1},{4,6},{5,7},{6,4},{7,5},{8,10},{9,11},{10,... | collective-permute-start | bytes 196616 | tf_op jit(solution)/shard_map/ppermute | solution.py:26
  18.0 0.0 collective-permute-done.2.refs_1_
  18.0 0.0 collective-permute-start.7
  18.0 0.0 copy-done
  18.1 4.6 %shard_map.84 = (bf16[96,128]{1,0:T(8,128)(2,1)S(1)}, bf16[2048,6144]{1,0:T(8,128)(2,1)S(1)}) custom-call(bf16[32,2048]{1,0:T(8,128)(2,1)S(1)} %get-tuple-element.34.normed, bf16[8,2048]{1,0:T(8,128)(2,1)S(1)} %bitcast.14, s32[2,32]{1,0:T(2,128)S(1)} %get-tuple-element.35.routes, bf16[2048,7168]{1,0:T(8,128)(2,1)} %bitcast.16), custom_call_target="tpu_custom_call" | custom-call | flops 1000000 | bytes 16777216 | tf_op jit(solution)/shard_map/pallas_call | solution.py:280
  22.7 0.0 collective-permute-done.3.refs_2_
  22.7 0.0 collective-permute-done.4.refs_3_
  22.7 0.0 collective-permute-done.5.refs_4_
  22.7 0.0 collective-permute-done.6.refs_5_
  22.7 0.0 collective-permute-done.7.refs_6_
  22.7 0.0 slice-done
  22.7 0.0 slice-done.1
  22.7 0.0 slice-done.2
  22.8 0.0 slice-done.3
  22.8 0.0 slice-done.4
  22.8 0.0 slice-done.5
  22.8 0.0 slice-done.6
  22.8 14.2 %shard_map.85 = (bf16[16,2048]{1,0:T(8,128)(2,1)S(1)}, bf16[16,2048]{1,0:T(8,128)(2,1)S(1)}, bf16[16,2048]{1,0:T(8,128)(2,1)S(1)}, bf16[16,2048]{1,0:T(8,128)(2,...) custom-call(bf16[16,2048]{1,0:T(8,128)(2,1)S(1)} %collective-permute, ...), custom_call_target="tpu_custom_call", output_to_operand_aliasing={{8}: (9, {}), {9}: (10, {})} | custom-call | flops 11274289152 | bytes 88080384 | tf_op jit(solution)/shard_map/pallas_call | solution.py:288
  37.0 4.2 %collective-permute-start.8 = (bf16[16,2048]{1,0:T(8,128)(2,1)S(1)}, bf16[16,2048]{1,0:T(8,128)(2,1)S(1)}, u32[]{:S(2)}, u32[]{:S(2)}) collective-permute-start(bf16[16,2048]{1,0:T(8,128)(2,1)S(1)} %get-tuple-element.47), channel_id=1, source_target_pairs={{0,7},{1,6},{2,5},{3,4},{4,3},{5,2},{6,1},{7,0},{8,15},{9,14},{10,... | collective-permute-start | bytes 196616 | tf_op jit(solution)/shard_map/ppermute | solution.py:26
  41.2 0.4 collective-permute-start.9
  41.5 1.3 %collective-permute-start.10 = (bf16[16,2048]{1,0:T(8,128)(2,1)S(1)}, bf16[16,2048]{1,0:T(8,128)(2,1)S(1)}, u32[]{:S(2)}, u32[]{:S(2)}) collective-permute-start(bf16[16,2048]{1,0:T(8,128)(2,1)S(1)} %get-tuple-element.49), channel_id=1, source_target_pairs={{0,5},{1,4},{2,7},{3,6},{4,1},{5,0},{6,3},{7,2},{8,13},{9,12},{10,... | collective-permute-start | bytes 196616 | tf_op jit(solution)/shard_map/ppermute | solution.py:26
  42.9 1.9 %collective-permute-start.11 = (bf16[16,2048]{1,0:T(8,128)(2,1)S(1)}, bf16[16,2048]{1,0:T(8,128)(2,1)S(1)}, u32[]{:S(2)}, u32[]{:S(2)}) collective-permute-start(bf16[16,2048]{1,0:T(8,128)(2,1)S(1)} %get-tuple-element.50), channel_id=1, source_target_pairs={{0,4},{1,5},{2,6},{3,7},{4,0},{5,1},{6,2},{7,3},{8,12},{9,13},{10,... | collective-permute-start | bytes 196616 | tf_op jit(solution)/shard_map/ppermute | solution.py:26
  44.7 1.2 %collective-permute-start.12 = (bf16[16,2048]{1,0:T(8,128)(2,1)S(1)}, bf16[16,2048]{1,0:T(8,128)(2,1)S(1)}, u32[]{:S(2)}, u32[]{:S(2)}) collective-permute-start(bf16[16,2048]{1,0:T(8,128)(2,1)S(1)} %get-tuple-element.51), channel_id=1, source_target_pairs={{0,3},{1,2},{2,1},{3,0},{4,7},{5,6},{6,5},{7,4},{8,11},{9,10},{10,... | collective-permute-start | bytes 196616 | tf_op jit(solution)/shard_map/ppermute | solution.py:26
  45.9 0.0 collective-permute-done.8.refs_0_
  45.9 3.1 %collective-permute-start.13 = (bf16[16,2048]{1,0:T(8,128)(2,1)S(1)}, bf16[16,2048]{1,0:T(8,128)(2,1)S(1)}, u32[]{:S(2)}, u32[]{:S(2)}) collective-permute-start(bf16[16,2048]{1,0:T(8,128)(2,1)S(1)} %get-tuple-element.52), channel_id=1, source_target_pairs={{0,2},{1,3},{2,0},{3,1},{4,6},{5,7},{6,4},{7,5},{8,10},{9,11},{10,... | collective-permute-start | bytes 196616 | tf_op jit(solution)/shard_map/ppermute | solution.py:26
  49.0 0.0 collective-permute-done.9.refs_1_
  49.0 0.0 collective-permute-start.14
  49.0 2.3 %collective-permute-done.10.refs_2_ = bf16[16,2048]{1,0:T(8,128)(2,1)S(1)} collective-permute-done((bf16[16,2048]{1,0:T(8,128)(2,1)S(1)}, bf16[16,2048]{1,0:T(8,128)(2,1)S(1)}, u32[]{:S(2)}, u32[]{:S(2)}) %collective-permute-start.10) | collective-permute-done | bytes 65568 | tf_op jit(solution)/shard_map/ppermute | solution.py:26
  51.3 1.2 %collective-permute-done.11.refs_3_ = bf16[16,2048]{1,0:T(8,128)(2,1)S(1)} collective-permute-done((bf16[16,2048]{1,0:T(8,128)(2,1)S(1)}, bf16[16,2048]{1,0:T(8,128)(2,1)S(1)}, u32[]{:S(2)}, u32[]{:S(2)}) %collective-permute-start.11) | collective-permute-done | bytes 65568 | tf_op jit(solution)/shard_map/ppermute | solution.py:26
  52.5 0.0 collective-permute-done.12.refs_4_
  52.5 0.4 collective-permute-done.13.refs_5_
  53.0 0.0 collective-permute-done.14.refs_6_
  53.0 0.9 %shard_map.86 = bf16[32,2048]{1,0:T(8,128)(2,1)} custom-call(bf16[32,2048]{1,0:T(8,128)(2,1)S(1)} %get-tuple-element.33.inputs, bf16[96,128]{1,0:T(8,128)(2,1)S(1)} %get-tuple-element.36.weights, bf16[16,2048]{1,0:T(8,128)(2,1)S(1)} %collective-permute-done.8.refs_0_, bf16[16,2048]{1,0:T(8,128)(2,1)S(1)} %collective-permute-done.9.refs_1_, ...), custom_call_target="tpu_custom_call" | custom-call | flops 100000000 | bytes 1000000 | tf_op jit(solution)/shard_map/pallas_call | solution.py:304
  (1 shorter events, 0.0 us)
Async XLA Ops:
  0.0 7.2 %collective-permute-start = (bf16[32,2048]{1,0:T(8,128)(2,1)}, bf16[32,2048]{1,0:T(8,128)(2,1)S(1)}, u32[]{:S(2)}, u32[]{:S(2)}) collective-permute-start(bf16[32,2048]{1,0:T(8,128)(2,1)} %bitcast.19), channel_id=1, source_target_pairs={{0,8},{8,16},{16,24},{1,9},{9,17},{17,25},{2,10},{10,18},{18,26},{... | collective-permute-start | bytes 393224 | tf_op jit(solution)/shard_map/ppermute | solution.py:21
  4.5 18.2 %slice-start = ((s8[29360128]{0:T(1024)(128)(4,1)}), s8[4194304]{0:T(1024)(128)(4,1)S(1)}, s32[]{:S(2)}) async-start(s8[29360128]{0:T(1024)(128)(4,1)} %bitcast.11), calls=%async_computation | async-start | bytes 8388608
  4.5 13.5 %copy-start = (bf16[1,2048,8]{1,2,0:T(8,128)(2,1)S(1)}, bf16[1,2048,8]{1,2,0:T(8,128)(2,1)}, u32[]{:S(2)}) copy-start(bf16[1,2048,8]{1,2,0:T(8,128)(2,1)} %param.12) | copy-start | bytes 98308
  4.5 18.2 %slice-start.1 = ((s8[29360128]{0:T(1024)(128)(4,1)}), s8[4194304]{0:T(1024)(128)(4,1)S(1)}, s32[]{:S(2)}) async-start(s8[29360128]{0:T(1024)(128)(4,1)} %bitcast.11), calls=%async_computation.1 | async-start | bytes 8388608
  4.5 18.2 %slice-start.2 = ((s8[29360128]{0:T(1024)(128)(4,1)}), s8[4194304]{0:T(1024)(128)(4,1)S(1)}, s32[]{:S(2)}) async-start(s8[29360128]{0:T(1024)(128)(4,1)} %bitcast.11), calls=%async_computation.2 | async-start | bytes 8388608
  4.5 18.2 %slice-start.3 = ((s8[29360128]{0:T(1024)(128)(4,1)}), s8[4194304]{0:T(1024)(128)(4,1)S(1)}, s32[]{:S(2)}) async-start(s8[29360128]{0:T(1024)(128)(4,1)} %bitcast.11), calls=%async_computation.3 | async-start | bytes 8388608
  4.6 18.2 %slice-start.4 = ((s8[29360128]{0:T(1024)(128)(4,1)}), s8[4194304]{0:T(1024)(128)(4,1)S(1)}, s32[]{:S(2)}) async-start(s8[29360128]{0:T(1024)(128)(4,1)} %bitcast.11), calls=%async_computation.4 | async-start | bytes 8388608
  4.6 18.2 %slice-start.5 = ((s8[29360128]{0:T(1024)(128)(4,1)}), s8[4194304]{0:T(1024)(128)(4,1)S(1)}, s32[]{:S(2)}) async-start(s8[29360128]{0:T(1024)(128)(4,1)} %bitcast.11), calls=%async_computation.5 | async-start | bytes 8388608
  4.6 18.2 %slice-start.6 = ((s8[29360128]{0:T(1024)(128)(4,1)}), s8[4194304]{0:T(1024)(128)(4,1)S(1)}, s32[]{:S(2)}) async-start(s8[29360128]{0:T(1024)(128)(4,1)} %bitcast.11), calls=%async_computation.6 | async-start | bytes 8388608
  7.6 8.8 %collective-permute-start.1 = (bf16[16,2048]{1,0:T(8,128)(2,1)S(1)}, bf16[16,2048]{1,0:T(8,128)(2,1)S(1)}, u32[]{:S(2)}, u32[]{:S(2)}) collective-permute-start(bf16[16,2048]{1,0:T(8,128)(2,1)S(1)} %get-tuple-element.37), channel_id=1, source_target_pairs={{0,7},{1,6},{2,5},{3,4},{4,3},{5,2},{6,1},{7,0},{8,15},{9,14},{10,... | collective-permute-start | bytes 196616 | tf_op jit(solution)/shard_map/ppermute | solution.py:26
  12.0 6.1 %collective-permute-start.2 = (bf16[16,2048]{1,0:T(8,128)(2,1)S(1)}, bf16[16,2048]{1,0:T(8,128)(2,1)S(1)}, u32[]{:S(2)}, u32[]{:S(2)}) collective-permute-start(bf16[16,2048]{1,0:T(8,128)(2,1)S(1)} %get-tuple-element.38), channel_id=1, source_target_pairs={{0,6},{1,7},{2,4},{3,5},{4,2},{5,3},{6,0},{7,1},{8,14},{9,15},{10,... | collective-permute-start | bytes 196616 | tf_op jit(solution)/shard_map/ppermute | solution.py:26
  12.0 10.7 %collective-permute-start.3 = (bf16[16,2048]{1,0:T(8,128)(2,1)S(1)}, bf16[16,2048]{1,0:T(8,128)(2,1)S(1)}, u32[]{:S(2)}, u32[]{:S(2)}) collective-permute-start(bf16[16,2048]{1,0:T(8,128)(2,1)S(1)} %get-tuple-element.39), channel_id=1, source_target_pairs={{0,5},{1,4},{2,7},{3,6},{4,1},{5,0},{6,3},{7,2},{8,13},{9,12},{10,... | collective-permute-start | bytes 196616 | tf_op jit(solution)/shard_map/ppermute | solution.py:26
  12.4 10.3 %collective-permute-start.4 = (bf16[16,2048]{1,0:T(8,128)(2,1)S(1)}, bf16[16,2048]{1,0:T(8,128)(2,1)S(1)}, u32[]{:S(2)}, u32[]{:S(2)}) collective-permute-start(bf16[16,2048]{1,0:T(8,128)(2,1)S(1)} %get-tuple-element.40), channel_id=1, source_target_pairs={{0,4},{1,5},{2,6},{3,7},{4,0},{5,1},{6,2},{7,3},{8,12},{9,13},{10,... | collective-permute-start | bytes 196616 | tf_op jit(solution)/shard_map/ppermute | solution.py:26
  14.4 8.3 %collective-permute-start.5 = (bf16[16,2048]{1,0:T(8,128)(2,1)S(1)}, bf16[16,2048]{1,0:T(8,128)(2,1)S(1)}, u32[]{:S(2)}, u32[]{:S(2)}) collective-permute-start(bf16[16,2048]{1,0:T(8,128)(2,1)S(1)} %get-tuple-element.41), channel_id=1, source_target_pairs={{0,3},{1,2},{2,1},{3,0},{4,7},{5,6},{6,5},{7,4},{8,11},{9,10},{10,... | collective-permute-start | bytes 196616 | tf_op jit(solution)/shard_map/ppermute | solution.py:26
  16.4 6.3 %collective-permute-start.6 = (bf16[16,2048]{1,0:T(8,128)(2,1)S(1)}, bf16[16,2048]{1,0:T(8,128)(2,1)S(1)}, u32[]{:S(2)}, u32[]{:S(2)}) collective-permute-start(bf16[16,2048]{1,0:T(8,128)(2,1)S(1)} %get-tuple-element.42), channel_id=1, source_target_pairs={{0,2},{1,3},{2,0},{3,1},{4,6},{5,7},{6,4},{7,5},{8,10},{9,11},{10,... | collective-permute-start | bytes 196616 | tf_op jit(solution)/shard_map/ppermute | solution.py:26
  18.0 4.7 %collective-permute-start.7 = (bf16[16,2048]{1,0:T(8,128)(2,1)S(1)}, bf16[16,2048]{1,0:T(8,128)(2,1)S(1)}, u32[]{:S(2)}, u32[]{:S(2)}) collective-permute-start(bf16[16,2048]{1,0:T(8,128)(2,1)S(1)} %get-tuple-element.43), channel_id=1, source_target_pairs={{0,1},{1,0},{2,3},{3,2},{4,5},{5,4},{6,7},{7,6},{8,9},{9,8},{10,11... | collective-permute-start | bytes 196616 | tf_op jit(solution)/shard_map/ppermute | solution.py:26
  37.0 8.9 %collective-permute-start.8 = (bf16[16,2048]{1,0:T(8,128)(2,1)S(1)}, bf16[16,2048]{1,0:T(8,128)(2,1)S(1)}, u32[]{:S(2)}, u32[]{:S(2)}) collective-permute-start(bf16[16,2048]{1,0:T(8,128)(2,1)S(1)} %get-tuple-element.47), channel_id=1, source_target_pairs={{0,7},{1,6},{2,5},{3,4},{4,3},{5,2},{6,1},{7,0},{8,15},{9,14},{10,... | collective-permute-start | bytes 196616 | tf_op jit(solution)/shard_map/ppermute | solution.py:26
  41.2 7.9 %collective-permute-start.9 = (bf16[16,2048]{1,0:T(8,128)(2,1)S(1)}, bf16[16,2048]{1,0:T(8,128)(2,1)S(1)}, u32[]{:S(2)}, u32[]{:S(2)}) collective-permute-start(bf16[16,2048]{1,0:T(8,128)(2,1)S(1)} %get-tuple-element.48), channel_id=1, source_target_pairs={{0,6},{1,7},{2,4},{3,5},{4,2},{5,3},{6,0},{7,1},{8,14},{9,15},{10,... | collective-permute-start | bytes 196616 | tf_op jit(solution)/shard_map/ppermute | solution.py:26
  41.5 9.8 %collective-permute-start.10 = (bf16[16,2048]{1,0:T(8,128)(2,1)S(1)}, bf16[16,2048]{1,0:T(8,128)(2,1)S(1)}, u32[]{:S(2)}, u32[]{:S(2)}) collective-permute-start(bf16[16,2048]{1,0:T(8,128)(2,1)S(1)} %get-tuple-element.49), channel_id=1, source_target_pairs={{0,5},{1,4},{2,7},{3,6},{4,1},{5,0},{6,3},{7,2},{8,13},{9,12},{10,... | collective-permute-start | bytes 196616 | tf_op jit(solution)/shard_map/ppermute | solution.py:26
  42.9 9.7 %collective-permute-start.11 = (bf16[16,2048]{1,0:T(8,128)(2,1)S(1)}, bf16[16,2048]{1,0:T(8,128)(2,1)S(1)}, u32[]{:S(2)}, u32[]{:S(2)}) collective-permute-start(bf16[16,2048]{1,0:T(8,128)(2,1)S(1)} %get-tuple-element.50), channel_id=1, source_target_pairs={{0,4},{1,5},{2,6},{3,7},{4,0},{5,1},{6,2},{7,3},{8,12},{9,13},{10,... | collective-permute-start | bytes 196616 | tf_op jit(solution)/shard_map/ppermute | solution.py:26
  44.7 7.8 %collective-permute-start.12 = (bf16[16,2048]{1,0:T(8,128)(2,1)S(1)}, bf16[16,2048]{1,0:T(8,128)(2,1)S(1)}, u32[]{:S(2)}, u32[]{:S(2)}) collective-permute-start(bf16[16,2048]{1,0:T(8,128)(2,1)S(1)} %get-tuple-element.51), channel_id=1, source_target_pairs={{0,3},{1,2},{2,1},{3,0},{4,7},{5,6},{6,5},{7,4},{8,11},{9,10},{10,... | collective-permute-start | bytes 196616 | tf_op jit(solution)/shard_map/ppermute | solution.py:26
  45.9 7.1 %collective-permute-start.13 = (bf16[16,2048]{1,0:T(8,128)(2,1)S(1)}, bf16[16,2048]{1,0:T(8,128)(2,1)S(1)}, u32[]{:S(2)}, u32[]{:S(2)}) collective-permute-start(bf16[16,2048]{1,0:T(8,128)(2,1)S(1)} %get-tuple-element.52), channel_id=1, source_target_pairs={{0,2},{1,3},{2,0},{3,1},{4,6},{5,7},{6,4},{7,5},{8,10},{9,11},{10,... | collective-permute-start | bytes 196616 | tf_op jit(solution)/shard_map/ppermute | solution.py:26
  49.0 4.0 %collective-permute-start.14 = (bf16[16,2048]{1,0:T(8,128)(2,1)S(1)}, bf16[16,2048]{1,0:T(8,128)(2,1)S(1)}, u32[]{:S(2)}, u32[]{:S(2)}) collective-permute-start(bf16[16,2048]{1,0:T(8,128)(2,1)S(1)} %get-tuple-element.53), channel_id=1, source_target_pairs={{0,1},{1,0},{2,3},{3,2},{4,5},{5,4},{6,7},{7,6},{8,9},{9,8},{10,11... | collective-permute-start | bytes 196616 | tf_op jit(solution)/shard_map/ppermute | solution.py:26

commit v4 on v3

--- a/solution.py
+++ b/solution.py
@@ -58,19 +58,15 @@
 ):
     pairs = ((routes, routes_here), (fresh, fresh_here), (gain, gain_here))
     copies = [pltpu.make_async_copy(a, b, sems.at[i]) for i, (a, b) in enumerate(pairs)]
+    fetch = pltpu.make_async_copy(up.at[:, : first.shape[1]], first, sems.at[len(pairs)])
     for copy in copies:
         copy.start()
-
-    @pl.when(tile_comes_late())
-    def _():
-        fetch = pltpu.make_async_copy(up.at[:, : first.shape[1]], first, sems.at[len(pairs)])
-        fetch.start()
-        fetch.wait()
-
+    pl.when(tile_comes_late())(fetch.start)
     copies[0].wait()
     placing[...] = slot_hits(routes_here[...], experts, capacity, None).astype(jnp.bfloat16)
     for copy in copies[1:]:
         copy.wait()
+    pl.when(tile_comes_late())(fetch.wait)
 
 
 def pack_kernel(received, fresh, gain, placing, inputs, normed, *blocks):
@@ -266,14 +262,14 @@
             pltpu.VMEM((width, CHUNK), bf16),
         ],
         [HBM] * 4,
-        flops=60 * 10**9,
+        flops=10**6,
         moved=10**6,
         scratch=[pltpu.SemaphoreType.DMA((4,))],
     )(*map(in_hbm, (fresh, chosen, norm_gain, w_up[0, 0])))
     tile = pltpu.VMEM((tokens, width), bf16)
     block = pltpu.VMEM((capacity, width), bf16)
     inputs, normed, *packed = call(
-        pack_kernel, [tile, tile] + [block] * experts, [VMEM] * 4, flops=10**7, moved=10**6
+        pack_kernel, [tile, tile] + [block] * experts, [VMEM] * 4, flops=60 * 10**9, moved=10**6
     )(*map(in_vmem, (received, fresh_here, gain_here, placing)))
     order = range(experts - 1, -1, -1)
     arrived = [swapped(packed[k], k) if k else packed[k] for k in order]

time: 54.1 us -> 54.3 us (level)
  starting transfers between devices: 27 us -> 27.6 us
    ppermute x14, starting transfers between devices: 22.5 us -> 23.1 us  [swapped(): return lax.ppermute(x, 'expert', [(i, i ^ k) for i in range(length)])]
where the time goes in v4:
time: 54.3 us; the launch traced here: 54.1 us
  starting transfers between devices  27.6 us (51%)
  Pallas kernels  22.4 us (41%)
  waiting for transfers between devices  3.85 us (7%)
    ppermute x14, starting transfers between devices, swapped(): return lax.ppermute(x, 'expert', [(i, i ^ k) for i in range(length)])  23.1 us
    pallas_call x1, Pallas kernels, one_expert_each(): call(functools.partial(ffn_kernel, experts, BAND, HEAD), [block] * expert...  14.2 us
    pallas_call x1, Pallas kernels, one_expert_each(): call(functools.partial(weigh_kernel, CHUNK, HEAD), [pltpu.VMEM((TERMS * t...  4.61 us
    ppermute x1, starting transfers between devices, passed_along(): return lax.ppermute(x, axis, pairs)  4.5 us
    ppermute x14, waiting for transfers between devices, swapped(): return lax.ppermute(x, 'expert', [(i, i ^ k) for i in range(length)])  3.84 us
    pallas_call x1, Pallas kernels, one_expert_each(): call(functools.partial(prepare_kernel, experts, capacity), [pltpu.VMEM((s...  2.34 us
  transfers between devices with their start and end apart: 15, of which 3 were waited for; matrix products, arithmetic and copies ran while one was open for 0% of the time, Pallas kernels for 13%

profile of v4, /device:TPU:1, one launch (start us, length us, event | category | flops | bytes accessed | tf_op | source)
XLA Modules:
  0.0 54.1 jit_solution(16916785248373459473)
XLA Ops:
  0.0 4.5 %collective-permute-start = (bf16[32,2048]{1,0:T(8,128)(2,1)}, bf16[32,2048]{1,0:T(8,128)(2,1)S(1)}, u32[]{:S(2)}, u32[]{:S(2)}) collective-permute-start(bf16[32,2048]{1,0:T(8,128)(2,1)} %bitcast.20), channel_id=1, source_target_pairs={{0,8},{8,16},{16,24},{1,9},{9,17},{17,25},{2,10},{10,18},{18,26},{... | collective-permute-start | bytes 393224 | tf_op jit(solution)/shard_map/ppermute | solution.py:21
  4.5 2.3 %shard_map.82 = (bf16[128,32]{1,0:T(8,128)(2,1)S(1)}, bf16[32,2048]{1,0:T(8,128)(2,1)S(1)}, s32[2,32]{1,0:T(2,128)S(1)}, f32[1,2048]{1,0:T(1,128)S(1)}, bf16[2048,1024]{1,0:T(8,128)(2,1)S(1)}) custom-call(bf16[32,2048]{1,0:T(8,128)(2,1)} %fresh.1, s32[2,32]{1,0:T(2,128)} %bitcast.19, f32[1,2048]{1,0:T(1,128)} %gain.1, bf16[2048,7168]{1,0:T(8,128)(2,1)} %bitcast.15), custom_call_target="tpu_custom_call" | custom-call | flops 1000000 | bytes 1000000 | tf_op jit(solution)/shard_map/pallas_call | solution.py:255
  6.8 0.0 collective-permute-done.received
  6.9 0.0 slice-start
  6.9 0.0 copy-start
  6.9 0.0 slice-start.1
  6.9 0.0 slice-start.2
  6.9 0.0 slice-start.3
  6.9 0.0 slice-start.4
  6.9 0.0 slice-start.5
  6.9 0.0 slice-start.6
  6.9 0.4 shard_map.83
  7.4 4.3 %collective-permute-start.1 = (bf16[16,2048]{1,0:T(8,128)(2,1)S(1)}, bf16[16,2048]{1,0:T(8,128)(2,1)S(1)}, u32[]{:S(2)}, u32[]{:S(2)}) collective-permute-start(bf16[16,2048]{1,0:T(8,128)(2,1)S(1)} %get-tuple-element.37), channel_id=1, source_target_pairs={{0,7},{1,6},{2,5},{3,4},{4,3},{5,2},{6,1},{7,0},{8,15},{9,14},{10,... | collective-permute-start | bytes 196616 | tf_op jit(solution)/shard_map/ppermute | solution.py:26
  11.7 0.0 collective-permute-start.2
  11.7 0.4 collective-permute-start.3
  12.1 2.0 %collective-permute-start.4 = (bf16[16,2048]{1,0:T(8,128)(2,1)S(1)}, bf16[16,2048]{1,0:T(8,128)(2,1)S(1)}, u32[]{:S(2)}, u32[]{:S(2)}) collective-permute-start(bf16[16,2048]{1,0:T(8,128)(2,1)S(1)} %get-tuple-element.40), channel_id=1, source_target_pairs={{0,4},{1,5},{2,6},{3,7},{4,0},{5,1},{6,2},{7,3},{8,12},{9,13},{10,... | collective-permute-start | bytes 196616 | tf_op jit(solution)/shard_map/ppermute | solution.py:26
  14.1 2.0 %collective-permute-start.5 = (bf16[16,2048]{1,0:T(8,128)(2,1)S(1)}, bf16[16,2048]{1,0:T(8,128)(2,1)S(1)}, u32[]{:S(2)}, u32[]{:S(2)}) collective-permute-start(bf16[16,2048]{1,0:T(8,128)(2,1)S(1)} %get-tuple-element.41), channel_id=1, source_target_pairs={{0,3},{1,2},{2,1},{3,0},{4,7},{5,6},{6,5},{7,4},{8,11},{9,10},{10,... | collective-permute-start | bytes 196616 | tf_op jit(solution)/shard_map/ppermute | solution.py:26
  16.2 0.0 collective-permute-done.1.refs_0_
  16.2 2.1 %collective-permute-start.6 = (bf16[16,2048]{1,0:T(8,128)(2,1)S(1)}, bf16[16,2048]{1,0:T(8,128)(2,1)S(1)}, u32[]{:S(2)}, u32[]{:S(2)}) collective-permute-start(bf16[16,2048]{1,0:T(8,128)(2,1)S(1)} %get-tuple-element.42), channel_id=1, source_target_pairs={{0,2},{1,3},{2,0},{3,1},{4,6},{5,7},{6,4},{7,5},{8,10},{9,11},{10,... | collective-permute-start | bytes 196616 | tf_op jit(solution)/shard_map/ppermute | solution.py:26
  18.3 0.0 collective-permute-done.2.refs_1_
  18.3 0.0 collective-permute-start.7
  18.3 0.0 copy-done
  18.3 4.6 %shard_map.84 = (bf16[96,128]{1,0:T(8,128)(2,1)S(1)}, bf16[2048,6144]{1,0:T(8,128)(2,1)S(1)}) custom-call(bf16[32,2048]{1,0:T(8,128)(2,1)S(1)} %get-tuple-element.34.normed, bf16[8,2048]{1,0:T(8,128)(2,1)S(1)} %bitcast.14, s32[2,32]{1,0:T(2,128)S(1)} %get-tuple-element.35.routes, bf16[2048,7168]{1,0:T(8,128)(2,1)} %bitcast.16), custom_call_target="tpu_custom_call" | custom-call | flops 1000000 | bytes 16777216 | tf_op jit(solution)/shard_map/pallas_call | solution.py:276
  22.9 0.0 collective-permute-done.3.refs_2_
  22.9 0.0 collective-permute-done.4.refs_3_
  22.9 0.0 collective-permute-done.5.refs_4_
  23.0 0.0 collective-permute-done.6.refs_5_
  23.0 0.0 collective-permute-done.7.refs_6_
  23.0 0.0 slice-done
  23.0 0.0 slice-done.1
  23.0 0.0 slice-done.2
  23.0 0.0 slice-done.3
  23.0 0.0 slice-done.4
  23.0 0.0 slice-done.5
  23.0 0.0 slice-done.6
  23.1 14.2 %shard_map.85 = (bf16[16,2048]{1,0:T(8,128)(2,1)S(1)}, bf16[16,2048]{1,0:T(8,128)(2,1)S(1)}, bf16[16,2048]{1,0:T(8,128)(2,1)S(1)}, bf16[16,2048]{1,0:T(8,128)(2,...) custom-call(bf16[16,2048]{1,0:T(8,128)(2,1)S(1)} %collective-permute, ...), custom_call_target="tpu_custom_call", output_to_operand_aliasing={{8}: (9, {}), {9}: (10, {})} | custom-call | flops 11274289152 | bytes 88080384 | tf_op jit(solution)/shard_map/pallas_call | solution.py:284
  37.2 3.9 %collective-permute-start.8 = (bf16[16,2048]{1,0:T(8,128)(2,1)S(1)}, bf16[16,2048]{1,0:T(8,128)(2,1)S(1)}, u32[]{:S(2)}, u32[]{:S(2)}) collective-permute-start(bf16[16,2048]{1,0:T(8,128)(2,1)S(1)} %get-tuple-element.47), channel_id=1, source_target_pairs={{0,7},{1,6},{2,5},{3,4},{4,3},{5,2},{6,1},{7,0},{8,15},{9,14},{10,... | collective-permute-start | bytes 196616 | tf_op jit(solution)/shard_map/ppermute | solution.py:26
  41.1 0.6 %collective-permute-start.9 = (bf16[16,2048]{1,0:T(8,128)(2,1)S(1)}, bf16[16,2048]{1,0:T(8,128)(2,1)S(1)}, u32[]{:S(2)}, u32[]{:S(2)}) collective-permute-start(bf16[16,2048]{1,0:T(8,128)(2,1)S(1)} %get-tuple-element.48), channel_id=1, source_target_pairs={{0,6},{1,7},{2,4},{3,5},{4,2},{5,3},{6,0},{7,1},{8,14},{9,15},{10,... | collective-permute-start | bytes 196616 | tf_op jit(solution)/shard_map/ppermute | solution.py:26
  41.7 1.2 %collective-permute-start.10 = (bf16[16,2048]{1,0:T(8,128)(2,1)S(1)}, bf16[16,2048]{1,0:T(8,128)(2,1)S(1)}, u32[]{:S(2)}, u32[]{:S(2)}) collective-permute-start(bf16[16,2048]{1,0:T(8,128)(2,1)S(1)} %get-tuple-element.49), channel_id=1, source_target_pairs={{0,5},{1,4},{2,7},{3,6},{4,1},{5,0},{6,3},{7,2},{8,13},{9,12},{10,... | collective-permute-start | bytes 196616 | tf_op jit(solution)/shard_map/ppermute | solution.py:26
  43.0 1.7 %collective-permute-start.11 = (bf16[16,2048]{1,0:T(8,128)(2,1)S(1)}, bf16[16,2048]{1,0:T(8,128)(2,1)S(1)}, u32[]{:S(2)}, u32[]{:S(2)}) collective-permute-start(bf16[16,2048]{1,0:T(8,128)(2,1)S(1)} %get-tuple-element.50), channel_id=1, source_target_pairs={{0,4},{1,5},{2,6},{3,7},{4,0},{5,1},{6,2},{7,3},{8,12},{9,13},{10,... | collective-permute-start | bytes 196616 | tf_op jit(solution)/shard_map/ppermute | solution.py:26
  44.7 1.2 %collective-permute-start.12 = (bf16[16,2048]{1,0:T(8,128)(2,1)S(1)}, bf16[16,2048]{1,0:T(8,128)(2,1)S(1)}, u32[]{:S(2)}, u32[]{:S(2)}) collective-permute-start(bf16[16,2048]{1,0:T(8,128)(2,1)S(1)} %get-tuple-element.51), channel_id=1, source_target_pairs={{0,3},{1,2},{2,1},{3,0},{4,7},{5,6},{6,5},{7,4},{8,11},{9,10},{10,... | collective-permute-start | bytes 196616 | tf_op jit(solution)/shard_map/ppermute | solution.py:26
  45.8 0.0 collective-permute-done.8.refs_0_
  45.8 3.5 %collective-permute-start.13 = (bf16[16,2048]{1,0:T(8,128)(2,1)S(1)}, bf16[16,2048]{1,0:T(8,128)(2,1)S(1)}, u32[]{:S(2)}, u32[]{:S(2)}) collective-permute-start(bf16[16,2048]{1,0:T(8,128)(2,1)S(1)} %get-tuple-element.52), channel_id=1, source_target_pairs={{0,2},{1,3},{2,0},{3,1},{4,6},{5,7},{6,4},{7,5},{8,10},{9,11},{10,... | collective-permute-start | bytes 196616 | tf_op jit(solution)/shard_map/ppermute | solution.py:26
  49.4 0.0 collective-permute-done.9.refs_1_
  49.4 0.0 collective-permute-start.14
  49.4 2.2 %collective-permute-done.10.refs_2_ = bf16[16,2048]{1,0:T(8,128)(2,1)S(1)} collective-permute-done((bf16[16,2048]{1,0:T(8,128)(2,1)S(1)}, bf16[16,2048]{1,0:T(8,128)(2,1)S(1)}, u32[]{:S(2)}, u32[]{:S(2)}) %collective-permute-start.10) | collective-permute-done | bytes 65568 | tf_op jit(solution)/shard_map/ppermute | solution.py:26
  51.5 1.1 %collective-permute-done.11.refs_3_ = bf16[16,2048]{1,0:T(8,128)(2,1)S(1)} collective-permute-done((bf16[16,2048]{1,0:T(8,128)(2,1)S(1)}, bf16[16,2048]{1,0:T(8,128)(2,1)S(1)}, u32[]{:S(2)}, u32[]{:S(2)}) %collective-permute-start.11) | collective-permute-done | bytes 65568 | tf_op jit(solution)/shard_map/ppermute | solution.py:26
  52.6 0.0 collective-permute-done.12.refs_4_
  52.6 0.6 %collective-permute-done.13.refs_5_ = bf16[16,2048]{1,0:T(8,128)(2,1)S(1)} collective-permute-done((bf16[16,2048]{1,0:T(8,128)(2,1)S(1)}, bf16[16,2048]{1,0:T(8,128)(2,1)S(1)}, u32[]{:S(2)}, u32[]{:S(2)}) %collective-permute-start.13) | collective-permute-done | bytes 65568 | tf_op jit(solution)/shard_map/ppermute | solution.py:26
  53.2 0.0 collective-permute-done.14.refs_6_
  53.2 0.9 %shard_map.86 = bf16[32,2048]{1,0:T(8,128)(2,1)} custom-call(bf16[32,2048]{1,0:T(8,128)(2,1)S(1)} %get-tuple-element.33.inputs, bf16[96,128]{1,0:T(8,128)(2,1)S(1)} %get-tuple-element.36.weights, bf16[16,2048]{1,0:T(8,128)(2,1)S(1)} %collective-permute-done.8.refs_0_, bf16[16,2048]{1,0:T(8,128)(2,1)S(1)} %collective-permute-done.9.refs_1_, ...), custom_call_target="tpu_custom_call" | custom-call | flops 100000000 | bytes 1000000 | tf_op jit(solution)/shard_map/pallas_call | solution.py:300
  (1 shorter events, 0.0 us)
Async XLA Ops:
  0.0 6.9 %collective-permute-start = (bf16[32,2048]{1,0:T(8,128)(2,1)}, bf16[32,2048]{1,0:T(8,128)(2,1)S(1)}, u32[]{:S(2)}, u32[]{:S(2)}) collective-permute-start(bf16[32,2048]{1,0:T(8,128)(2,1)} %bitcast.20), channel_id=1, source_target_pairs={{0,8},{8,16},{16,24},{1,9},{9,17},{17,25},{2,10},{10,18},{18,26},{... | collective-permute-start | bytes 393224 | tf_op jit(solution)/shard_map/ppermute | solution.py:21
  6.9 16.1 %slice-start = ((s8[29360128]{0:T(1024)(128)(4,1)}), s8[4194304]{0:T(1024)(128)(4,1)S(1)}, s32[]{:S(2)}) async-start(s8[29360128]{0:T(1024)(128)(4,1)} %bitcast.11), calls=%async_computation | async-start | bytes 8388608
  6.9 11.4 %copy-start = (bf16[1,2048,8]{1,2,0:T(8,128)(2,1)S(1)}, bf16[1,2048,8]{1,2,0:T(8,128)(2,1)}, u32[]{:S(2)}) copy-start(bf16[1,2048,8]{1,2,0:T(8,128)(2,1)} %param.12) | copy-start | bytes 98308
  6.9 16.1 %slice-start.1 = ((s8[29360128]{0:T(1024)(128)(4,1)}), s8[4194304]{0:T(1024)(128)(4,1)S(1)}, s32[]{:S(2)}) async-start(s8[29360128]{0:T(1024)(128)(4,1)} %bitcast.11), calls=%async_computation.1 | async-start | bytes 8388608
  6.9 16.1 %slice-start.2 = ((s8[29360128]{0:T(1024)(128)(4,1)}), s8[4194304]{0:T(1024)(128)(4,1)S(1)}, s32[]{:S(2)}) async-start(s8[29360128]{0:T(1024)(128)(4,1)} %bitcast.11), calls=%async_computation.2 | async-start | bytes 8388608
  6.9 16.1 %slice-start.3 = ((s8[29360128]{0:T(1024)(128)(4,1)}), s8[4194304]{0:T(1024)(128)(4,1)S(1)}, s32[]{:S(2)}) async-start(s8[29360128]{0:T(1024)(128)(4,1)} %bitcast.11), calls=%async_computation.3 | async-start | bytes 8388608
  6.9 16.1 %slice-start.4 = ((s8[29360128]{0:T(1024)(128)(4,1)}), s8[4194304]{0:T(1024)(128)(4,1)S(1)}, s32[]{:S(2)}) async-start(s8[29360128]{0:T(1024)(128)(4,1)} %bitcast.11), calls=%async_computation.4 | async-start | bytes 8388608
  6.9 16.1 %slice-start.5 = ((s8[29360128]{0:T(1024)(128)(4,1)}), s8[4194304]{0:T(1024)(128)(4,1)S(1)}, s32[]{:S(2)}) async-start(s8[29360128]{0:T(1024)(128)(4,1)} %bitcast.11), calls=%async_computation.5 | async-start | bytes 8388608
  6.9 16.1 %slice-start.6 = ((s8[29360128]{0:T(1024)(128)(4,1)}), s8[4194304]{0:T(1024)(128)(4,1)S(1)}, s32[]{:S(2)}) async-start(s8[29360128]{0:T(1024)(128)(4,1)} %bitcast.11), calls=%async_computation.6 | async-start | bytes 8388608
  7.4 8.8 %collective-permute-start.1 = (bf16[16,2048]{1,0:T(8,128)(2,1)S(1)}, bf16[16,2048]{1,0:T(8,128)(2,1)S(1)}, u32[]{:S(2)}, u32[]{:S(2)}) collective-permute-start(bf16[16,2048]{1,0:T(8,128)(2,1)S(1)} %get-tuple-element.37), channel_id=1, source_target_pairs={{0,7},{1,6},{2,5},{3,4},{4,3},{5,2},{6,1},{7,0},{8,15},{9,14},{10,... | collective-permute-start | bytes 196616 | tf_op jit(solution)/shard_map/ppermute | solution.py:26
  11.7 6.6 %collective-permute-start.2 = (bf16[16,2048]{1,0:T(8,128)(2,1)S(1)}, bf16[16,2048]{1,0:T(8,128)(2,1)S(1)}, u32[]{:S(2)}, u32[]{:S(2)}) collective-permute-start(bf16[16,2048]{1,0:T(8,128)(2,1)S(1)} %get-tuple-element.38), channel_id=1, source_target_pairs={{0,6},{1,7},{2,4},{3,5},{4,2},{5,3},{6,0},{7,1},{8,14},{9,15},{10,... | collective-permute-start | bytes 196616 | tf_op jit(solution)/shard_map/ppermute | solution.py:26
  11.7 11.2 %collective-permute-start.3 = (bf16[16,2048]{1,0:T(8,128)(2,1)S(1)}, bf16[16,2048]{1,0:T(8,128)(2,1)S(1)}, u32[]{:S(2)}, u32[]{:S(2)}) collective-permute-start(bf16[16,2048]{1,0:T(8,128)(2,1)S(1)} %get-tuple-element.39), channel_id=1, source_target_pairs={{0,5},{1,4},{2,7},{3,6},{4,1},{5,0},{6,3},{7,2},{8,13},{9,12},{10,... | collective-permute-start | bytes 196616 | tf_op jit(solution)/shard_map/ppermute | solution.py:26
  12.1 10.8 %collective-permute-start.4 = (bf16[16,2048]{1,0:T(8,128)(2,1)S(1)}, bf16[16,2048]{1,0:T(8,128)(2,1)S(1)}, u32[]{:S(2)}, u32[]{:S(2)}) collective-permute-start(bf16[16,2048]{1,0:T(8,128)(2,1)S(1)} %get-tuple-element.40), channel_id=1, source_target_pairs={{0,4},{1,5},{2,6},{3,7},{4,0},{5,1},{6,2},{7,3},{8,12},{9,13},{10,... | collective-permute-start | bytes 196616 | tf_op jit(solution)/shard_map/ppermute | solution.py:26
  14.1 8.8 %collective-permute-start.5 = (bf16[16,2048]{1,0:T(8,128)(2,1)S(1)}, bf16[16,2048]{1,0:T(8,128)(2,1)S(1)}, u32[]{:S(2)}, u32[]{:S(2)}) collective-permute-start(bf16[16,2048]{1,0:T(8,128)(2,1)S(1)} %get-tuple-element.41), channel_id=1, source_target_pairs={{0,3},{1,2},{2,1},{3,0},{4,7},{5,6},{6,5},{7,4},{8,11},{9,10},{10,... | collective-permute-start | bytes 196616 | tf_op jit(solution)/shard_map/ppermute | solution.py:26
  16.2 6.8 %collective-permute-start.6 = (bf16[16,2048]{1,0:T(8,128)(2,1)S(1)}, bf16[16,2048]{1,0:T(8,128)(2,1)S(1)}, u32[]{:S(2)}, u32[]{:S(2)}) collective-permute-start(bf16[16,2048]{1,0:T(8,128)(2,1)S(1)} %get-tuple-element.42), channel_id=1, source_target_pairs={{0,2},{1,3},{2,0},{3,1},{4,6},{5,7},{6,4},{7,5},{8,10},{9,11},{10,... | collective-permute-start | bytes 196616 | tf_op jit(solution)/shard_map/ppermute | solution.py:26
  18.3 4.7 %collective-permute-start.7 = (bf16[16,2048]{1,0:T(8,128)(2,1)S(1)}, bf16[16,2048]{1,0:T(8,128)(2,1)S(1)}, u32[]{:S(2)}, u32[]{:S(2)}) collective-permute-start(bf16[16,2048]{1,0:T(8,128)(2,1)S(1)} %get-tuple-element.43), channel_id=1, source_target_pairs={{0,1},{1,0},{2,3},{3,2},{4,5},{5,4},{6,7},{7,6},{8,9},{9,8},{10,11... | collective-permute-start | bytes 196616 | tf_op jit(solution)/shard_map/ppermute | solution.py:26
  37.2 8.6 %collective-permute-start.8 = (bf16[16,2048]{1,0:T(8,128)(2,1)S(1)}, bf16[16,2048]{1,0:T(8,128)(2,1)S(1)}, u32[]{:S(2)}, u32[]{:S(2)}) collective-permute-start(bf16[16,2048]{1,0:T(8,128)(2,1)S(1)} %get-tuple-element.47), channel_id=1, source_target_pairs={{0,7},{1,6},{2,5},{3,4},{4,3},{5,2},{6,1},{7,0},{8,15},{9,14},{10,... | collective-permute-start | bytes 196616 | tf_op jit(solution)/shard_map/ppermute | solution.py:26
  41.1 8.3 %collective-permute-start.9 = (bf16[16,2048]{1,0:T(8,128)(2,1)S(1)}, bf16[16,2048]{1,0:T(8,128)(2,1)S(1)}, u32[]{:S(2)}, u32[]{:S(2)}) collective-permute-start(bf16[16,2048]{1,0:T(8,128)(2,1)S(1)} %get-tuple-element.48), channel_id=1, source_target_pairs={{0,6},{1,7},{2,4},{3,5},{4,2},{5,3},{6,0},{7,1},{8,14},{9,15},{10,... | collective-permute-start | bytes 196616 | tf_op jit(solution)/shard_map/ppermute | solution.py:26
  41.7 9.8 %collective-permute-start.10 = (bf16[16,2048]{1,0:T(8,128)(2,1)S(1)}, bf16[16,2048]{1,0:T(8,128)(2,1)S(1)}, u32[]{:S(2)}, u32[]{:S(2)}) collective-permute-start(bf16[16,2048]{1,0:T(8,128)(2,1)S(1)} %get-tuple-element.49), channel_id=1, source_target_pairs={{0,5},{1,4},{2,7},{3,6},{4,1},{5,0},{6,3},{7,2},{8,13},{9,12},{10,... | collective-permute-start | bytes 196616 | tf_op jit(solution)/shard_map/ppermute | solution.py:26
  43.0 9.7 %collective-permute-start.11 = (bf16[16,2048]{1,0:T(8,128)(2,1)S(1)}, bf16[16,2048]{1,0:T(8,128)(2,1)S(1)}, u32[]{:S(2)}, u32[]{:S(2)}) collective-permute-start(bf16[16,2048]{1,0:T(8,128)(2,1)S(1)} %get-tuple-element.50), channel_id=1, source_target_pairs={{0,4},{1,5},{2,6},{3,7},{4,0},{5,1},{6,2},{7,3},{8,12},{9,13},{10,... | collective-permute-start | bytes 196616 | tf_op jit(solution)/shard_map/ppermute | solution.py:26
  44.7 8.0 %collective-permute-start.12 = (bf16[16,2048]{1,0:T(8,128)(2,1)S(1)}, bf16[16,2048]{1,0:T(8,128)(2,1)S(1)}, u32[]{:S(2)}, u32[]{:S(2)}) collective-permute-start(bf16[16,2048]{1,0:T(8,128)(2,1)S(1)} %get-tuple-element.51), channel_id=1, source_target_pairs={{0,3},{1,2},{2,1},{3,0},{4,7},{5,6},{6,5},{7,4},{8,11},{9,10},{10,... | collective-permute-start | bytes 196616 | tf_op jit(solution)/shard_map/ppermute | solution.py:26
  45.8 7.3 %collective-permute-start.13 = (bf16[16,2048]{1,0:T(8,128)(2,1)S(1)}, bf16[16,2048]{1,0:T(8,128)(2,1)S(1)}, u32[]{:S(2)}, u32[]{:S(2)}) collective-permute-start(bf16[16,2048]{1,0:T(8,128)(2,1)S(1)} %get-tuple-element.52), channel_id=1, source_target_pairs={{0,2},{1,3},{2,0},{3,1},{4,6},{5,7},{6,4},{7,5},{8,10},{9,11},{10,... | collective-permute-start | bytes 196616 | tf_op jit(solution)/shard_map/ppermute | solution.py:26
  49.4 3.8 %collective-permute-start.14 = (bf16[16,2048]{1,0:T(8,128)(2,1)S(1)}, bf16[16,2048]{1,0:T(8,128)(2,1)S(1)}, u32[]{:S(2)}, u32[]{:S(2)}) collective-permute-start(bf16[16,2048]{1,0:T(8,128)(2,1)S(1)} %get-tuple-element.53), channel_id=1, source_target_pairs={{0,1},{1,0},{2,3},{3,2},{4,5},{5,4},{6,7},{7,6},{8,9},{9,8},{10,11... | collective-permute-start | bytes 196616 | tf_op jit(solution)/shard_map/ppermute | solution.py:26

commit v5 on v4

--- a/solution.py
+++ b/solution.py
@@ -50,7 +50,7 @@
 
 def tile_comes_late():
     section = lax.axis_index("pipe")
-    return (section > 0) & (section < lax.axis_size("pipe") - 1)
+    return (section > 1) & (section < lax.axis_size("pipe") - 1)
 
 
 def prepare_kernel(

time: 54.3 us -> 54.1 us (level)
  starting transfers between devices: 27.6 us -> 26.9 us
  waiting for transfers between devices: 3.85 us -> 4.47 us
    pallas_call x1, Pallas kernels: 2.34 us -> 0.96 us  [one_expert_each(): call(functools.partial(prepare_kernel, experts, capacity), [pltpu.VMEM((s...]
    ppermute x1, waiting for transfers between devices: 0.01 us -> 1.27 us  [passed_along(): return lax.ppermute(x, axis, pairs)]
    pallas_call x1, Pallas kernels: 4.61 us -> 5.81 us  [one_expert_each(): call(functools.partial(weigh_kernel, CHUNK, HEAD), [pltpu.VMEM((TERMS * t...]
    ppermute x14, waiting for transfers between devices: 3.84 us -> 3.2 us  [swapped(): return lax.ppermute(x, 'expert', [(i, i ^ k) for i in range(length)])]
    ppermute x14, starting transfers between devices: 23.1 us -> 22.4 us  [swapped(): return lax.ppermute(x, 'expert', [(i, i ^ k) for i in range(length)])]
  transfers between devices with their start and end apart: 15 -> 15, of which waited for: 3 -> 4; matrix products, arithmetic and copies ran while one was open for 0% -> 0% of each run, Pallas kernels for 13% -> 13%
where the time goes in v5:
time: 54.1 us; the launch traced here: 53.9 us
  starting transfers between devices  26.9 us (50%)
  Pallas kernels  22.3 us (41%)
  waiting for transfers between devices  4.47 us (8%)
    ppermute x14, starting transfers between devices, swapped(): return lax.ppermute(x, 'expert', [(i, i ^ k) for i in range(length)])  22.4 us
    pallas_call x1, Pallas kernels, one_expert_each(): call(functools.partial(ffn_kernel, experts, BAND, HEAD), [block] * expert...  14.2 us
    pallas_call x1, Pallas kernels, one_expert_each(): call(functools.partial(weigh_kernel, CHUNK, HEAD), [pltpu.VMEM((TERMS * t...  5.81 us
    ppermute x1, starting transfers between devices, passed_along(): return lax.ppermute(x, axis, pairs)  4.5 us
    ppermute x14, waiting for transfers between devices, swapped(): return lax.ppermute(x, 'expert', [(i, i ^ k) for i in range(length)])  3.2 us
    ppermute x1, waiting for transfers between devices, passed_along(): return lax.ppermute(x, axis, pairs)  1.27 us
  transfers between devices with their start and end apart: 15, of which 4 were waited for; matrix products, arithmetic and copies ran while one was open for 0% of the time, Pallas kernels for 13%

profile of v5, /device:TPU:1, one launch (start us, length us, event | category | flops | bytes accessed | tf_op | source)
XLA Modules:
  0.0 53.9 jit_solution(16548163774686540029)
XLA Ops:
  0.0 4.5 %collective-permute-start = (bf16[32,2048]{1,0:T(8,128)(2,1)}, bf16[32,2048]{1,0:T(8,128)(2,1)S(1)}, u32[]{:S(2)}, u32[]{:S(2)}) collective-permute-start(bf16[32,2048]{1,0:T(8,128)(2,1)} %bitcast.20), channel_id=1, source_target_pairs={{0,8},{8,16},{16,24},{1,9},{9,17},{17,25},{2,10},{10,18},{18,26},{... | collective-permute-start | bytes 393224 | tf_op jit(solution)/shard_map/ppermute | solution.py:21
  4.5 1.0 %shard_map.82 = (bf16[128,32]{1,0:T(8,128)(2,1)S(1)}, bf16[32,2048]{1,0:T(8,128)(2,1)S(1)}, s32[2,32]{1,0:T(2,128)S(1)}, f32[1,2048]{1,0:T(1,128)S(1)}, bf16[2048,1024]{1,0:T(8,128)(2,1)S(1)}) custom-call(bf16[32,2048]{1,0:T(8,128)(2,1)} %fresh.1, s32[2,32]{1,0:T(2,128)} %bitcast.19, f32[1,2048]{1,0:T(1,128)} %gain.1, bf16[2048,7168]{1,0:T(8,128)(2,1)} %bitcast.15), custom_call_target="tpu_custom_call" | custom-call | flops 1000000 | bytes 1000000 | tf_op jit(solution)/shard_map/pallas_call | solution.py:255
  5.5 1.3 %collective-permute-done.received = bf16[32,2048]{1,0:T(8,128)(2,1)S(1)} collective-permute-done((bf16[32,2048]{1,0:T(8,128)(2,1)}, bf16[32,2048]{1,0:T(8,128)(2,1)S(1)}, u32[]{:S(2)}, u32[]{:S(2)}) %collective-permute-start) | collective-permute-done | bytes 131104 | tf_op jit(solution)/shard_map/ppermute | solution.py:21
  6.7 0.0 slice-start
  6.7 0.0 copy-start
  6.8 0.0 slice-start.1
  6.8 0.0 slice-start.2
  6.8 0.0 slice-start.3
  6.8 0.0 slice-start.4
  6.8 0.0 slice-start.5
  6.8 0.0 slice-start.6
  6.8 0.4 shard_map.83
  7.2 4.3 %collective-permute-start.1 = (bf16[16,2048]{1,0:T(8,128)(2,1)S(1)}, bf16[16,2048]{1,0:T(8,128)(2,1)S(1)}, u32[]{:S(2)}, u32[]{:S(2)}) collective-permute-start(bf16[16,2048]{1,0:T(8,128)(2,1)S(1)} %get-tuple-element.37), channel_id=1, source_target_pairs={{0,7},{1,6},{2,5},{3,4},{4,3},{5,2},{6,1},{7,0},{8,15},{9,14},{10,... | collective-permute-start | bytes 196616 | tf_op jit(solution)/shard_map/ppermute | solution.py:26
  11.6 0.0 collective-permute-start.2
  11.6 0.4 collective-permute-start.3
  11.9 2.0 %collective-permute-start.4 = (bf16[16,2048]{1,0:T(8,128)(2,1)S(1)}, bf16[16,2048]{1,0:T(8,128)(2,1)S(1)}, u32[]{:S(2)}, u32[]{:S(2)}) collective-permute-start(bf16[16,2048]{1,0:T(8,128)(2,1)S(1)} %get-tuple-element.40), channel_id=1, source_target_pairs={{0,4},{1,5},{2,6},{3,7},{4,0},{5,1},{6,2},{7,3},{8,12},{9,13},{10,... | collective-permute-start | bytes 196616 | tf_op jit(solution)/shard_map/ppermute | solution.py:26
  14.0 2.0 %collective-permute-start.5 = (bf16[16,2048]{1,0:T(8,128)(2,1)S(1)}, bf16[16,2048]{1,0:T(8,128)(2,1)S(1)}, u32[]{:S(2)}, u32[]{:S(2)}) collective-permute-start(bf16[16,2048]{1,0:T(8,128)(2,1)S(1)} %get-tuple-element.41), channel_id=1, source_target_pairs={{0,3},{1,2},{2,1},{3,0},{4,7},{5,6},{6,5},{7,4},{8,11},{9,10},{10,... | collective-permute-start | bytes 196616 | tf_op jit(solution)/shard_map/ppermute | solution.py:26
  16.0 0.0 collective-permute-done.1.refs_0_
  16.0 2.2 %collective-permute-start.6 = (bf16[16,2048]{1,0:T(8,128)(2,1)S(1)}, bf16[16,2048]{1,0:T(8,128)(2,1)S(1)}, u32[]{:S(2)}, u32[]{:S(2)}) collective-permute-start(bf16[16,2048]{1,0:T(8,128)(2,1)S(1)} %get-tuple-element.42), channel_id=1, source_target_pairs={{0,2},{1,3},{2,0},{3,1},{4,6},{5,7},{6,4},{7,5},{8,10},{9,11},{10,... | collective-permute-start | bytes 196616 | tf_op jit(solution)/shard_map/ppermute | solution.py:26
  18.2 0.0 collective-permute-done.2.refs_1_
  18.2 0.0 collective-permute-start.7
  18.2 0.0 copy-done
  18.2 5.8 %shard_map.84 = (bf16[96,128]{1,0:T(8,128)(2,1)S(1)}, bf16[2048,6144]{1,0:T(8,128)(2,1)S(1)}) custom-call(bf16[32,2048]{1,0:T(8,128)(2,1)S(1)} %get-tuple-element.34.normed, bf16[8,2048]{1,0:T(8,128)(2,1)S(1)} %bitcast.14, s32[2,32]{1,0:T(2,128)S(1)} %get-tuple-element.35.routes, bf16[2048,7168]{1,0:T(8,128)(2,1)} %bitcast.16), custom_call_target="tpu_custom_call" | custom-call | flops 1000000 | bytes 16777216 | tf_op jit(solution)/shard_map/pallas_call | solution.py:276
  24.0 0.0 collective-permute-done.3.refs_2_
  24.1 0.0 collective-permute-done.4.refs_3_
  24.1 0.0 collective-permute-done.5.refs_4_
  24.1 0.0 collective-permute-done.6.refs_5_
  24.1 0.0 collective-permute-done.7.refs_6_
  24.1 0.0 slice-done
  24.1 0.0 slice-done.1
  24.1 0.0 slice-done.2
  24.1 0.0 slice-done.3
  24.1 0.0 slice-done.4
  24.1 0.0 slice-done.5
  24.2 0.0 slice-done.6
  24.2 14.2 %shard_map.85 = (bf16[16,2048]{1,0:T(8,128)(2,1)S(1)}, bf16[16,2048]{1,0:T(8,128)(2,1)S(1)}, bf16[16,2048]{1,0:T(8,128)(2,1)S(1)}, bf16[16,2048]{1,0:T(8,128)(2,...) custom-call(bf16[16,2048]{1,0:T(8,128)(2,1)S(1)} %collective-permute, ...), custom_call_target="tpu_custom_call", output_to_operand_aliasing={{8}: (9, {}), {9}: (10, {})} | custom-call | flops 11274289152 | bytes 88080384 | tf_op jit(solution)/shard_map/pallas_call | solution.py:284
  38.4 4.0 %collective-permute-start.8 = (bf16[16,2048]{1,0:T(8,128)(2,1)S(1)}, bf16[16,2048]{1,0:T(8,128)(2,1)S(1)}, u32[]{:S(2)}, u32[]{:S(2)}) collective-permute-start(bf16[16,2048]{1,0:T(8,128)(2,1)S(1)} %get-tuple-element.47), channel_id=1, source_target_pairs={{0,7},{1,6},{2,5},{3,4},{4,3},{5,2},{6,1},{7,0},{8,15},{9,14},{10,... | collective-permute-start | bytes 196616 | tf_op jit(solution)/shard_map/ppermute | solution.py:26
  42.3 0.5 collective-permute-start.9
  42.9 1.2 %collective-permute-start.10 = (bf16[16,2048]{1,0:T(8,128)(2,1)S(1)}, bf16[16,2048]{1,0:T(8,128)(2,1)S(1)}, u32[]{:S(2)}, u32[]{:S(2)}) collective-permute-start(bf16[16,2048]{1,0:T(8,128)(2,1)S(1)} %get-tuple-element.49), channel_id=1, source_target_pairs={{0,5},{1,4},{2,7},{3,6},{4,1},{5,0},{6,3},{7,2},{8,13},{9,12},{10,... | collective-permute-start | bytes 196616 | tf_op jit(solution)/shard_map/ppermute | solution.py:26
  44.1 1.8 %collective-permute-start.11 = (bf16[16,2048]{1,0:T(8,128)(2,1)S(1)}, bf16[16,2048]{1,0:T(8,128)(2,1)S(1)}, u32[]{:S(2)}, u32[]{:S(2)}) collective-permute-start(bf16[16,2048]{1,0:T(8,128)(2,1)S(1)} %get-tuple-element.50), channel_id=1, source_target_pairs={{0,4},{1,5},{2,6},{3,7},{4,0},{5,1},{6,2},{7,3},{8,12},{9,13},{10,... | collective-permute-start | bytes 196616 | tf_op jit(solution)/shard_map/ppermute | solution.py:26
  45.9 1.2 %collective-permute-start.12 = (bf16[16,2048]{1,0:T(8,128)(2,1)S(1)}, bf16[16,2048]{1,0:T(8,128)(2,1)S(1)}, u32[]{:S(2)}, u32[]{:S(2)}) collective-permute-start(bf16[16,2048]{1,0:T(8,128)(2,1)S(1)} %get-tuple-element.51), channel_id=1, source_target_pairs={{0,3},{1,2},{2,1},{3,0},{4,7},{5,6},{6,5},{7,4},{8,11},{9,10},{10,... | collective-permute-start | bytes 196616 | tf_op jit(solution)/shard_map/ppermute | solution.py:26
  47.1 0.0 collective-permute-done.8.refs_0_
  47.1 2.6 %collective-permute-start.13 = (bf16[16,2048]{1,0:T(8,128)(2,1)S(1)}, bf16[16,2048]{1,0:T(8,128)(2,1)S(1)}, u32[]{:S(2)}, u32[]{:S(2)}) collective-permute-start(bf16[16,2048]{1,0:T(8,128)(2,1)S(1)} %get-tuple-element.52), channel_id=1, source_target_pairs={{0,2},{1,3},{2,0},{3,1},{4,6},{5,7},{6,4},{7,5},{8,10},{9,11},{10,... | collective-permute-start | bytes 196616 | tf_op jit(solution)/shard_map/ppermute | solution.py:26
  49.6 0.0 collective-permute-done.9.refs_1_
  49.6 0.1 collective-permute-start.14
  49.8 1.8 %collective-permute-done.10.refs_2_ = bf16[16,2048]{1,0:T(8,128)(2,1)S(1)} collective-permute-done((bf16[16,2048]{1,0:T(8,128)(2,1)S(1)}, bf16[16,2048]{1,0:T(8,128)(2,1)S(1)}, u32[]{:S(2)}, u32[]{:S(2)}) %collective-permute-start.10) | collective-permute-done | bytes 65568 | tf_op jit(solution)/shard_map/ppermute | solution.py:26
  51.6 1.1 %collective-permute-done.11.refs_3_ = bf16[16,2048]{1,0:T(8,128)(2,1)S(1)} collective-permute-done((bf16[16,2048]{1,0:T(8,128)(2,1)S(1)}, bf16[16,2048]{1,0:T(8,128)(2,1)S(1)}, u32[]{:S(2)}, u32[]{:S(2)}) %collective-permute-start.11) | collective-permute-done | bytes 65568 | tf_op jit(solution)/shard_map/ppermute | solution.py:26
  52.7 0.0 collective-permute-done.12.refs_4_
  52.7 0.3 collective-permute-done.13.refs_5_
  52.9 0.0 collective-permute-done.14.refs_6_
  53.0 0.9 %shard_map.86 = bf16[32,2048]{1,0:T(8,128)(2,1)} custom-call(bf16[32,2048]{1,0:T(8,128)(2,1)S(1)} %get-tuple-element.33.inputs, bf16[96,128]{1,0:T(8,128)(2,1)S(1)} %get-tuple-element.36.weights, bf16[16,2048]{1,0:T(8,128)(2,1)S(1)} %collective-permute-done.8.refs_0_, bf16[16,2048]{1,0:T(8,128)(2,1)S(1)} %collective-permute-done.9.refs_1_, ...), custom_call_target="tpu_custom_call" | custom-call | flops 100000000 | bytes 1000000 | tf_op jit(solution)/shard_map/pallas_call | solution.py:300
  (1 shorter events, 0.0 us)
Async XLA Ops:
  0.0 6.7 %collective-permute-start = (bf16[32,2048]{1,0:T(8,128)(2,1)}, bf16[32,2048]{1,0:T(8,128)(2,1)S(1)}, u32[]{:S(2)}, u32[]{:S(2)}) collective-permute-start(bf16[32,2048]{1,0:T(8,128)(2,1)} %bitcast.20), channel_id=1, source_target_pairs={{0,8},{8,16},{16,24},{1,9},{9,17},{17,25},{2,10},{10,18},{18,26},{... | collective-permute-start | bytes 393224 | tf_op jit(solution)/shard_map/ppermute | solution.py:21
  6.7 17.4 %slice-start = ((s8[29360128]{0:T(1024)(128)(4,1)}), s8[4194304]{0:T(1024)(128)(4,1)S(1)}, s32[]{:S(2)}) async-start(s8[29360128]{0:T(1024)(128)(4,1)} %bitcast.11), calls=%async_computation | async-start | bytes 8388608
  6.7 11.5 %copy-start = (bf16[1,2048,8]{1,2,0:T(8,128)(2,1)S(1)}, bf16[1,2048,8]{1,2,0:T(8,128)(2,1)}, u32[]{:S(2)}) copy-start(bf16[1,2048,8]{1,2,0:T(8,128)(2,1)} %param.12) | copy-start | bytes 98308
  6.8 17.4 %slice-start.1 = ((s8[29360128]{0:T(1024)(128)(4,1)}), s8[4194304]{0:T(1024)(128)(4,1)S(1)}, s32[]{:S(2)}) async-start(s8[29360128]{0:T(1024)(128)(4,1)} %bitcast.11), calls=%async_computation.1 | async-start | bytes 8388608
  6.8 17.4 %slice-start.2 = ((s8[29360128]{0:T(1024)(128)(4,1)}), s8[4194304]{0:T(1024)(128)(4,1)S(1)}, s32[]{:S(2)}) async-start(s8[29360128]{0:T(1024)(128)(4,1)} %bitcast.11), calls=%async_computation.2 | async-start | bytes 8388608
  6.8 17.4 %slice-start.3 = ((s8[29360128]{0:T(1024)(128)(4,1)}), s8[4194304]{0:T(1024)(128)(4,1)S(1)}, s32[]{:S(2)}) async-start(s8[29360128]{0:T(1024)(128)(4,1)} %bitcast.11), calls=%async_computation.3 | async-start | bytes 8388608
  6.8 17.4 %slice-start.4 = ((s8[29360128]{0:T(1024)(128)(4,1)}), s8[4194304]{0:T(1024)(128)(4,1)S(1)}, s32[]{:S(2)}) async-start(s8[29360128]{0:T(1024)(128)(4,1)} %bitcast.11), calls=%async_computation.4 | async-start | bytes 8388608
  6.8 17.4 %slice-start.5 = ((s8[29360128]{0:T(1024)(128)(4,1)}), s8[4194304]{0:T(1024)(128)(4,1)S(1)}, s32[]{:S(2)}) async-start(s8[29360128]{0:T(1024)(128)(4,1)} %bitcast.11), calls=%async_computation.5 | async-start | bytes 8388608
  6.8 17.4 %slice-start.6 = ((s8[29360128]{0:T(1024)(128)(4,1)}), s8[4194304]{0:T(1024)(128)(4,1)S(1)}, s32[]{:S(2)}) async-start(s8[29360128]{0:T(1024)(128)(4,1)} %bitcast.11), calls=%async_computation.6 | async-start | bytes 8388608
  7.2 8.8 %collective-permute-start.1 = (bf16[16,2048]{1,0:T(8,128)(2,1)S(1)}, bf16[16,2048]{1,0:T(8,128)(2,1)S(1)}, u32[]{:S(2)}, u32[]{:S(2)}) collective-permute-start(bf16[16,2048]{1,0:T(8,128)(2,1)S(1)} %get-tuple-element.37), channel_id=1, source_target_pairs={{0,7},{1,6},{2,5},{3,4},{4,3},{5,2},{6,1},{7,0},{8,15},{9,14},{10,... | collective-permute-start | bytes 196616 | tf_op jit(solution)/shard_map/ppermute | solution.py:26
  11.6 6.7 %collective-permute-start.2 = (bf16[16,2048]{1,0:T(8,128)(2,1)S(1)}, bf16[16,2048]{1,0:T(8,128)(2,1)S(1)}, u32[]{:S(2)}, u32[]{:S(2)}) collective-permute-start(bf16[16,2048]{1,0:T(8,128)(2,1)S(1)} %get-tuple-element.38), channel_id=1, source_target_pairs={{0,6},{1,7},{2,4},{3,5},{4,2},{5,3},{6,0},{7,1},{8,14},{9,15},{10,... | collective-permute-start | bytes 196616 | tf_op jit(solution)/shard_map/ppermute | solution.py:26
  11.6 12.5 %collective-permute-start.3 = (bf16[16,2048]{1,0:T(8,128)(2,1)S(1)}, bf16[16,2048]{1,0:T(8,128)(2,1)S(1)}, u32[]{:S(2)}, u32[]{:S(2)}) collective-permute-start(bf16[16,2048]{1,0:T(8,128)(2,1)S(1)} %get-tuple-element.39), channel_id=1, source_target_pairs={{0,5},{1,4},{2,7},{3,6},{4,1},{5,0},{6,3},{7,2},{8,13},{9,12},{10,... | collective-permute-start | bytes 196616 | tf_op jit(solution)/shard_map/ppermute | solution.py:26
  11.9 12.1 %collective-permute-start.4 = (bf16[16,2048]{1,0:T(8,128)(2,1)S(1)}, bf16[16,2048]{1,0:T(8,128)(2,1)S(1)}, u32[]{:S(2)}, u32[]{:S(2)}) collective-permute-start(bf16[16,2048]{1,0:T(8,128)(2,1)S(1)} %get-tuple-element.40), channel_id=1, source_target_pairs={{0,4},{1,5},{2,6},{3,7},{4,0},{5,1},{6,2},{7,3},{8,12},{9,13},{10,... | collective-permute-start | bytes 196616 | tf_op jit(solution)/shard_map/ppermute | solution.py:26
  14.0 10.1 %collective-permute-start.5 = (bf16[16,2048]{1,0:T(8,128)(2,1)S(1)}, bf16[16,2048]{1,0:T(8,128)(2,1)S(1)}, u32[]{:S(2)}, u32[]{:S(2)}) collective-permute-start(bf16[16,2048]{1,0:T(8,128)(2,1)S(1)} %get-tuple-element.41), channel_id=1, source_target_pairs={{0,3},{1,2},{2,1},{3,0},{4,7},{5,6},{6,5},{7,4},{8,11},{9,10},{10,... | collective-permute-start | bytes 196616 | tf_op jit(solution)/shard_map/ppermute | solution.py:26
  16.0 8.1 %collective-permute-start.6 = (bf16[16,2048]{1,0:T(8,128)(2,1)S(1)}, bf16[16,2048]{1,0:T(8,128)(2,1)S(1)}, u32[]{:S(2)}, u32[]{:S(2)}) collective-permute-start(bf16[16,2048]{1,0:T(8,128)(2,1)S(1)} %get-tuple-element.42), channel_id=1, source_target_pairs={{0,2},{1,3},{2,0},{3,1},{4,6},{5,7},{6,4},{7,5},{8,10},{9,11},{10,... | collective-permute-start | bytes 196616 | tf_op jit(solution)/shard_map/ppermute | solution.py:26
  18.2 5.9 %collective-permute-start.7 = (bf16[16,2048]{1,0:T(8,128)(2,1)S(1)}, bf16[16,2048]{1,0:T(8,128)(2,1)S(1)}, u32[]{:S(2)}, u32[]{:S(2)}) collective-permute-start(bf16[16,2048]{1,0:T(8,128)(2,1)S(1)} %get-tuple-element.43), channel_id=1, source_target_pairs={{0,1},{1,0},{2,3},{3,2},{4,5},{5,4},{6,7},{7,6},{8,9},{9,8},{10,11... | collective-permute-start | bytes 196616 | tf_op jit(solution)/shard_map/ppermute | solution.py:26
  38.4 8.7 %collective-permute-start.8 = (bf16[16,2048]{1,0:T(8,128)(2,1)S(1)}, bf16[16,2048]{1,0:T(8,128)(2,1)S(1)}, u32[]{:S(2)}, u32[]{:S(2)}) collective-permute-start(bf16[16,2048]{1,0:T(8,128)(2,1)S(1)} %get-tuple-element.47), channel_id=1, source_target_pairs={{0,7},{1,6},{2,5},{3,4},{4,3},{5,2},{6,1},{7,0},{8,15},{9,14},{10,... | collective-permute-start | bytes 196616 | tf_op jit(solution)/shard_map/ppermute | solution.py:26
  42.3 7.3 %collective-permute-start.9 = (bf16[16,2048]{1,0:T(8,128)(2,1)S(1)}, bf16[16,2048]{1,0:T(8,128)(2,1)S(1)}, u32[]{:S(2)}, u32[]{:S(2)}) collective-permute-start(bf16[16,2048]{1,0:T(8,128)(2,1)S(1)} %get-tuple-element.48), channel_id=1, source_target_pairs={{0,6},{1,7},{2,4},{3,5},{4,2},{5,3},{6,0},{7,1},{8,14},{9,15},{10,... | collective-permute-start | bytes 196616 | tf_op jit(solution)/shard_map/ppermute | solution.py:26
  42.9 8.7 %collective-permute-start.10 = (bf16[16,2048]{1,0:T(8,128)(2,1)S(1)}, bf16[16,2048]{1,0:T(8,128)(2,1)S(1)}, u32[]{:S(2)}, u32[]{:S(2)}) collective-permute-start(bf16[16,2048]{1,0:T(8,128)(2,1)S(1)} %get-tuple-element.49), channel_id=1, source_target_pairs={{0,5},{1,4},{2,7},{3,6},{4,1},{5,0},{6,3},{7,2},{8,13},{9,12},{10,... | collective-permute-start | bytes 196616 | tf_op jit(solution)/shard_map/ppermute | solution.py:26
  44.1 8.6 %collective-permute-start.11 = (bf16[16,2048]{1,0:T(8,128)(2,1)S(1)}, bf16[16,2048]{1,0:T(8,128)(2,1)S(1)}, u32[]{:S(2)}, u32[]{:S(2)}) collective-permute-start(bf16[16,2048]{1,0:T(8,128)(2,1)S(1)} %get-tuple-element.50), channel_id=1, source_target_pairs={{0,4},{1,5},{2,6},{3,7},{4,0},{5,1},{6,2},{7,3},{8,12},{9,13},{10,... | collective-permute-start | bytes 196616 | tf_op jit(solution)/shard_map/ppermute | solution.py:26
  45.9 6.8 %collective-permute-start.12 = (bf16[16,2048]{1,0:T(8,128)(2,1)S(1)}, bf16[16,2048]{1,0:T(8,128)(2,1)S(1)}, u32[]{:S(2)}, u32[]{:S(2)}) collective-permute-start(bf16[16,2048]{1,0:T(8,128)(2,1)S(1)} %get-tuple-element.51), channel_id=1, source_target_pairs={{0,3},{1,2},{2,1},{3,0},{4,7},{5,6},{6,5},{7,4},{8,11},{9,10},{10,... | collective-permute-start | bytes 196616 | tf_op jit(solution)/shard_map/ppermute | solution.py:26
  47.1 5.9 %collective-permute-start.13 = (bf16[16,2048]{1,0:T(8,128)(2,1)S(1)}, bf16[16,2048]{1,0:T(8,128)(2,1)S(1)}, u32[]{:S(2)}, u32[]{:S(2)}) collective-permute-start(bf16[16,2048]{1,0:T(8,128)(2,1)S(1)} %get-tuple-element.52), channel_id=1, source_target_pairs={{0,2},{1,3},{2,0},{3,1},{4,6},{5,7},{6,4},{7,5},{8,10},{9,11},{10,... | collective-permute-start | bytes 196616 | tf_op jit(solution)/shard_map/ppermute | solution.py:26
  49.6 3.3 %collective-permute-start.14 = (bf16[16,2048]{1,0:T(8,128)(2,1)S(1)}, bf16[16,2048]{1,0:T(8,128)(2,1)S(1)}, u32[]{:S(2)}, u32[]{:S(2)}) collective-permute-start(bf16[16,2048]{1,0:T(8,128)(2,1)S(1)} %get-tuple-element.53), channel_id=1, source_target_pairs={{0,1},{1,0},{2,3},{3,2},{4,5},{5,4},{6,7},{7,6},{8,9},{9,8},{10,11... | collective-permute-start | bytes 196616 | tf_op jit(solution)/shard_map/ppermute | solution.py:26
